TPU v7x, 512 devices: a whole 4x4x16 slice. The times are simulated.
512 devices in a mesh: gx: 4 (over x), gy: 16 (over z_lo, y), gz: 8 (over z_hi, core).
Axes of the slice: x: 4, y: 4, z: 16 (z_hi: 4, z_lo: 4; z = z_hi * 4 + z_lo), core: 2. Of those that a mesh axis runs over, the one named last changes fastest.
Arguments:
- bin_mass: float32 [32, 128, 128, 64], P('gx', 'gy', 'gz'), may hold values from 0.02 to 2
- courant: float32 [3, 32, 128, 128], P(None, 'gx', 'gy', 'gz'), may hold values from 0.05 to 0.3
- sub_courant: float32 [64], replicated, may hold values from 0.3 to 0.9
- fall_steps: int32 [64], replicated, may hold values from 1 to 24, as said below
- frag_gain: bfloat16 [4096, 64], replicated, may hold values from -0.01171875 to 0.01171875
- collide: bfloat16 [64, 64], replicated, may hold values from 0.0019989014 to 0.019897461
Outputs:
- updated_mass: float32 [32, 128, 128, 64], P('gx', 'gy', 'gz')
- rainfall: float32 [32, 128, 64], P('gx', ('gy', 'gz'))
Inputs may be any that keep to these rules, and one draw needn't show every extreme that they name: `fall_steps`: some bin takes 24 substeps.
All inputs are finite; a program needn't handle non-finite values.
Results may differ from a plain program's by a relative error of at most 0.003.
Values sent between devices are 32-bit elements; how exact they have to be, the bound alone decides.
A program may use at most 64 MiB of HBM per device.

v0:
```python
import jax
import jax.numpy as jnp
from jax import lax
from jax.sharding import PartitionSpec as P

SUBS = 24


EPS = 1e-06


def extended(cells, sides, width):
    for axis, dim in sides:
        count = lax.axis_size(axis)
        ends = count - 1
        head = lax.slice_in_dim(cells, 0, width, axis=dim)
        tail = lax.slice_in_dim(cells, cells.shape[dim] - width, cells.shape[dim], axis=dim)
        cells = jnp.concatenate(
            [
                lax.ppermute(tail, axis, [(i, (i + 1) % count) for i in range(ends)]),
                cells,
                lax.ppermute(head, axis, [((i + 1) % count, i) for i in range(ends)]),
            ],
            axis=dim,
        )
    return cells


def face_estimate(far_left, near_left, centre, near_right, far_right):
    left_poly = (2.0 * far_left - 7.0 * near_left + 11.0 * centre) / 6.0
    mid_poly = (-near_left + 5.0 * centre + 2.0 * near_right) / 6.0
    right_poly = (2.0 * centre + 5.0 * near_right - far_right) / 6.0
    left_smooth = 13.0 / 12.0 * jnp.square(far_left - 2.0 * near_left + centre) + 0.25 * jnp.square(
        far_left - 4.0 * near_left + 3.0 * centre
    )
    mid_smooth = 13.0 / 12.0 * jnp.square(
        near_left - 2.0 * centre + near_right
    ) + 0.25 * jnp.square(near_left - near_right)
    right_smooth = 13.0 / 12.0 * jnp.square(
        centre - 2.0 * near_right + far_right
    ) + 0.25 * jnp.square(3.0 * centre - 4.0 * near_right + far_right)
    left_weight = 0.1 / jnp.square(EPS + left_smooth)
    mid_weight = 0.6 / jnp.square(EPS + mid_smooth)
    right_weight = 0.3 / jnp.square(EPS + right_smooth)
    return (left_weight * left_poly + mid_weight * mid_poly + right_weight * right_poly) / (
        left_weight + mid_weight + right_weight
    )


def advect(padded, wind_pad):
    change_sum = None
    for axis_d in range(3):
        values_d = padded
        speed_d = wind_pad[axis_d]
        for other in range(3):
            if other != axis_d:
                values_d = lax.slice_in_dim(values_d, 3, values_d.shape[other] - 3, axis=other)
                speed_d = lax.slice_in_dim(speed_d, 1, speed_d.shape[other] - 1, axis=other)
        length = padded.shape[axis_d] - 6
        stencil = [lax.slice_in_dim(values_d, k, k + length + 1, axis=axis_d) for k in range(5)]
        estimate = face_estimate(stencil[0], stencil[1], stencil[2], stencil[3], stencil[4])
        face_speed = 0.5 * (
            lax.slice_in_dim(speed_d, 0, length + 1, axis=axis_d)
            + lax.slice_in_dim(speed_d, 1, length + 2, axis=axis_d)
        )
        face_flux = face_speed[..., None] * estimate
        difference = lax.slice_in_dim(face_flux, 1, length + 1, axis=axis_d) - lax.slice_in_dim(
            face_flux, 0, length, axis=axis_d
        )
        change_sum = -difference if change_sum is None else change_sum - difference
    return change_sum


def zero_layer(current):
    return jnp.zeros_like(current[:, :, :1])


def settle(mass, sub_courant, fall_steps, top_layer):

    def substep(step, carry):
        current, rainfall = carry
        fall_rate = jnp.where(step < fall_steps, sub_courant, jnp.float32(0.0))
        upper_cell = jnp.concatenate([current[:, :, 1:], top_layer(current)], axis=2)
        rainfall = rainfall + fall_rate * current[:, :, 0]
        current = current + fall_rate * (upper_cell - current)
        return (current, rainfall)

    empty = jnp.zeros((mass.shape[0], mass.shape[1], mass.shape[3]), jnp.float32)
    return lax.fori_loop(0, SUBS, substep, (mass, empty))


def breakup(settled, frag_gain, collide):
    bins = settled.shape[-1]
    flat = settled.reshape(-1, bins)
    count = flat.shape[0]
    block = 512

    def block_rows(rows_in):
        rounded = rows_in.astype(jnp.bfloat16)
        widened = rounded.astype(jnp.float32)
        pair_terms = (
            (widened[:, :, None] * widened[:, None, :])
            .reshape(rows_in.shape[0], bins * bins)
            .astype(jnp.bfloat16)
        )
        gained = jnp.dot(pair_terms, frag_gain, preferred_element_type=jnp.float32)
        breakup_loss = jnp.dot(rounded, collide, preferred_element_type=jnp.float32)
        return rows_in + gained - rows_in * breakup_loss

    blocks = flat.reshape(count // block, block, bins)
    return lax.map(block_rows, blocks).reshape(settled.shape)


def per_device(bin_mass, courant, sub_courant, fall_steps, frag_gain, collide):
    wind_pad = extended(courant, (("gx", 1), ("gy", 2), ("gz", 3)), 1)

    def section_tendency(values):
        padded = extended(values, (("gx", 0), ("gy", 1), ("gz", 2)), 3)
        return advect(padded, wind_pad)

    section_one = bin_mass + section_tendency(bin_mass)
    advected = 0.5 * bin_mass + 0.5 * (section_one + section_tendency(section_one))
    settled, rainfall = settle(
        lax.all_to_all(advected, "gz", split_axis=1, concat_axis=2, tiled=True),
        sub_courant,
        fall_steps,
        zero_layer,
    )
    updated_columns, rainfall = (breakup(settled, frag_gain, collide), rainfall)
    updated_mass = lax.all_to_all(updated_columns, "gz", split_axis=2, concat_axis=1, tiled=True)
    return (updated_mass, rainfall)


def solution(mesh):
    in_specs = (P("gx", "gy", "gz", None), P(None, "gx", "gy", "gz"), P(), P(), P(), P())
    out_specs = (P("gx", "gy", "gz", None), P("gx", ("gy", "gz"), None))
    return jax.shard_map(
        per_device, mesh=mesh, in_specs=in_specs, out_specs=out_specs, check_vma=False
    )
```

profile of v0, /device:TPU:67, one launch (start us, length us, event | category | flops | bytes accessed | tf_op | source)
XLA Modules:
  0.0 219.2 jit_solution(8227725181255863566)
XLA Ops:
  1.4 3.1 %collective-permute-start = (f32[3,1,8,16]{3,2,1,0:T(8,128)S(1)}, f32[3,1,8,16]{3,2,1,0:T(8,128)S(1)}, u32[]{:S(2)}, u32[]{:S(2)}) collective-permute-start(f32[3,1,8,16]{3,2,1,0:T(8,128)S(1)} %get-tuple-element.257), channel_id=1, source_target_pairs={{0,128},{128,256},{256,384},{1,129},{129,257},{257,385},{2,130},{1... | collective-permute-start | bytes 4616 | tf_op jit(solution)/shard_map/ppermute | solution.py:20
  4.5 2.2 collective-permute-start.1
  9.0 4.2 %collective-permute-start.3 = (f32[3,10,1,16]{3,2,1,0:T(1,128)S(1)}, f32[3,10,1,16]{3,2,1,0:T(1,128)S(1)}, u32[]{:S(2)}, u32[]{:S(2)}) collective-permute-start(f32[3,10,1,16]{3,2,1,0:T(1,128)S(1)} %get-tuple-element.255), channel_id=1, source_target_pairs={{8,0},{16,8},{24,16},{32,24},{40,32},{48,40},{56,48},{64,56},{72,6... | collective-permute-start | bytes 5768 | tf_op jit(solution)/shard_map/ppermute | solution.py:22
  13.2 1.9 collective-permute-start.2
  15.1 4.6 %collective-permute-done.2 = f32[3,10,1,16]{3,2,1,0:T(1,128)S(1)} collective-permute-done((f32[3,10,1,16]{3,2,1,0:T(1,128)S(1)}, f32[3,10,1,16]{3,2,1,0:T(1,128)S(1)}, u32[]{:S(2)}, u32[]{:S(2)}) %collective-permute-start.2) | collective-permute-done | bytes 1952 | tf_op jit(solution)/shard_map/ppermute | solution.py:20
  20.0 5.4 %collective-permute-start.5 = (f32[3,10,10,1]{3,2,1,0:T(8,128)S(1)}, f32[3,10,10,1]{3,2,1,0:T(8,128)S(1)}, u32[]{:S(2)}, u32[]{:S(2)}) collective-permute-start(f32[3,10,10,1]{3,2,1,0:T(8,128)S(1)} %get-tuple-element.249), channel_id=1, source_target_pairs={{1,0},{2,1},{3,2},{4,3},{5,4},{6,5},{7,6},{9,8},{10,9},{11,10},{12... | collective-permute-start | bytes 3608 | tf_op jit(solution)/shard_map/ppermute | solution.py:22
  25.4 8.7 %collective-permute-start.4 = (f32[3,10,10,1]{3,2,1,0:T(8,128)S(1)}, f32[3,10,10,1]{3,2,1,0:T(8,128)S(1)}, u32[]{:S(2)}, u32[]{:S(2)}) collective-permute-start(f32[3,10,10,1]{3,2,1,0:T(8,128)S(1)} %get-tuple-element.248), channel_id=1, source_target_pairs={{0,1},{1,2},{2,3},{3,4},{4,5},{5,6},{6,7},{8,9},{9,10},{10,11},{11... | collective-permute-start | bytes 3608 | tf_op jit(solution)/shard_map/ppermute | solution.py:20
  34.3 2.8 %collective-permute-start.6 = (f32[3,8,16,64]{3,1,2,0:T(8,128)S(1)}, f32[3,8,16,64]{3,1,2,0:T(8,128)S(1)}, u32[]{:S(2)}, u32[]{:S(2)}) collective-permute-start(f32[3,8,16,64]{3,1,2,0:T(8,128)S(1)} %copy.114), channel_id=1, source_target_pairs={{0,128},{128,256},{256,384},{1,129},{129,257},{257,385},{2,130},{1... | collective-permute-start | bytes 294920 | tf_op jit(solution)/shard_map/ppermute | solution.py:20
  37.2 2.5 %collective-permute-start.7 = (f32[3,8,16,64]{3,1,2,0:T(8,128)S(1)}, f32[3,8,16,64]{3,1,2,0:T(8,128)S(1)}, u32[]{:S(2)}, u32[]{:S(2)}) collective-permute-start(f32[3,8,16,64]{3,1,2,0:T(8,128)S(1)} %copy.115), channel_id=1, source_target_pairs={{128,0},{256,128},{384,256},{129,1},{257,129},{385,257},{130,2},{2... | collective-permute-start | bytes 294920 | tf_op jit(solution)/shard_map/ppermute | solution.py:22
  43.9 1.9 collective-permute-start.9
  45.8 3.4 %collective-permute-start.8 = (f32[14,3,16,64]{3,2,1,0:T(8,128)S(1)}, f32[14,3,16,64]{3,2,1,0:T(8,128)S(1)}, u32[]{:S(2)}, u32[]{:S(2)}) collective-permute-start(f32[14,3,16,64]{3,2,1,0:T(8,128)S(1)} %copy.84), channel_id=1, source_target_pairs={{0,8},{8,16},{16,24},{24,32},{32,40},{40,48},{48,56},{56,64},{64,7... | collective-permute-start | bytes 516104 | tf_op jit(solution)/shard_map/ppermute | solution.py:20
  52.0 3.9 %collective-permute-done.8 = f32[14,3,16,64]{3,2,1,0:T(8,128)S(1)} collective-permute-done((f32[14,3,16,64]{3,2,1,0:T(8,128)S(1)}, f32[14,3,16,64]{3,2,1,0:T(8,128)S(1)}, u32[]{:S(2)}, u32[]{:S(2)}) %collective-permute-start.8) | collective-permute-done | bytes 172064 | tf_op jit(solution)/shard_map/ppermute | solution.py:20
  56.3 1.9 collective-permute-start.11
  58.2 8.8 %collective-permute-start.10 = (f32[14,14,3,64]{3,1,2,0:T(8,128)S(1)}, f32[14,14,3,64]{3,1,2,0:T(8,128)S(1)}, u32[]{:S(2)}, u32[]{:S(2)}) collective-permute-start(f32[14,14,3,64]{3,1,2,0:T(8,128)S(1)} %get-tuple-element.231), channel_id=1, source_target_pairs={{0,1},{1,2},{2,3},{3,4},{4,5},{5,6},{6,7},{8,9},{9,10},{10,11},{11... | collective-permute-start | bytes 451592 | tf_op jit(solution)/shard_map/ppermute | solution.py:20
  67.1 3.1 %divide_multiply_fusion.1 = f32[8,9,16,64]{3,1,2,0:T(8,128)S(1)} fusion(f32[14,3,16,64]{3,1,2,0:T(4,128)S(1)} %copy.87, f32[14,8,16,64]{3,1,2,0:T(8,128)S(1)} %get-tuple-element.253, f32[14,3,16,64]{3,1,2,0:T(4,128)S(1)} %copy.85, f32[8,9,16]{1,2,0:T(8,128)S(1)} %copy.82), kind=kLoop, calls=%fused_computation.27 | loop fusion | flops 5160960 | bytes 1102336 | tf_op jit(solution)/shard_map/mul | solution.py:66
  70.1 7.4 %collective-permute-done.11 = f32[14,14,3,64]{3,1,2,0:T(8,128)S(1)} collective-permute-done((f32[14,14,3,64]{3,1,2,0:T(8,128)S(1)}, f32[14,14,3,64]{3,1,2,0:T(8,128)S(1)}, u32[]{:S(2)}, u32[]{:S(2)}) %collective-permute-start.11) | collective-permute-done | bytes 150560 | tf_op jit(solution)/shard_map/ppermute | solution.py:22
  77.6 2.7 %divide_multiply_fusion.5 = f32[8,8,17,64]{3,1,2,0:T(8,128)S(1)} fusion(f32[14,14,3,64]{3,1,2,0:T(8,128)S(1)} %collective-permute-done.11, f32[14,3,16,64]{3,1,2,0:T(4,128)S(1)} %copy.87, f32[14,8,16,64]{3,1,2,0:T(8,128)S(1)} %get-tuple-element.253, f32[14,3,16,64]{3,1,2,0:T(4,128)S(1)} %copy.85, f32[14,14,3,64]{3,1,2,0:T(8,128)S(1)} %collective-permute-done.10, ...), kind=kLoop, calls=%fused_computation.91 | loop fusion | flops 5570560 | bytes 1386752 | tf_op jit(solution)/shard_map/mul | solution.py:66
  80.7 1.9 collective-permute-start.13
  82.6 3.4 %collective-permute-start.12 = (f32[3,8,16,64]{3,1,2,0:T(8,128)S(1)}, f32[3,8,16,64]{3,1,2,0:T(8,128)S(1)}, u32[]{:S(2)}, u32[]{:S(2)}) collective-permute-start(f32[3,8,16,64]{3,1,2,0:T(8,128)S(1)} %get-tuple-element.241), channel_id=1, source_target_pairs={{0,128},{128,256},{256,384},{1,129},{129,257},{257,385},{2,130},{1... | collective-permute-start | bytes 294920 | tf_op jit(solution)/shard_map/ppermute | solution.py:20
  87.4 1.9 collective-permute-done.12
  91.6 3.4 %collective-permute-start.14 = (f32[14,3,16,64]{3,2,1,0:T(8,128)S(1)}, f32[14,3,16,64]{3,2,1,0:T(8,128)S(1)}, u32[]{:S(2)}, u32[]{:S(2)}) collective-permute-start(f32[14,3,16,64]{3,2,1,0:T(8,128)S(1)} %copy.92), channel_id=1, source_target_pairs={{0,8},{8,16},{16,24},{24,32},{32,40},{40,48},{48,56},{56,64},{64,7... | collective-permute-start | bytes 516104 | tf_op jit(solution)/shard_map/ppermute | solution.py:20
  96.5 3.0 %collective-permute-done.15 = f32[14,3,16,64]{3,2,1,0:T(8,128)S(1)} collective-permute-done((f32[14,3,16,64]{3,2,1,0:T(8,128)S(1)}, f32[14,3,16,64]{3,2,1,0:T(8,128)S(1)}, u32[]{:S(2)}, u32[]{:S(2)}) %collective-permute-start.15) | collective-permute-done | bytes 172064 | tf_op jit(solution)/shard_map/ppermute | solution.py:22
  99.6 2.1 collective-permute-done.14
  104.0 10.5 %collective-permute-start.16 = (f32[14,14,3,64]{3,1,2,0:T(8,128)S(1)}, f32[14,14,3,64]{3,1,2,0:T(8,128)S(1)}, u32[]{:S(2)}, u32[]{:S(2)}) collective-permute-start(f32[14,14,3,64]{3,1,2,0:T(8,128)S(1)} %get-tuple-element.229), channel_id=1, source_target_pairs={{0,1},{1,2},{2,3},{3,4},{4,5},{5,6},{6,7},{8,9},{9,10},{10,11},{11... | collective-permute-start | bytes 451592 | tf_op jit(solution)/shard_map/ppermute | solution.py:20
  115.0 2.6 %divide_multiply_fusion = f32[8,9,16,64]{3,1,2,0:T(8,128)S(1)} fusion(f32[14,11,16,64]{3,1,2,0:T(8,128)S(1)} %get-tuple-element.234, f32[14,11,16,64]{3,1,2,0:T(8,128)S(1)} %get-tuple-element.233, f32[8,9,16]{1,2,0:T(8,128)S(1)} %copy.82), kind=kLoop, calls=%fused_computation.26 | loop fusion | flops 4792320 | bytes 1774080 | tf_op jit(solution)/shard_map/mul | solution.py:66
  117.6 5.9 %collective-permute-done.17 = f32[14,14,3,64]{3,1,2,0:T(8,128)S(1)} collective-permute-done((f32[14,14,3,64]{3,1,2,0:T(8,128)S(1)}, f32[14,14,3,64]{3,1,2,0:T(8,128)S(1)}, u32[]{:S(2)}, u32[]{:S(2)}) %collective-permute-start.17) | collective-permute-done | bytes 150560 | tf_op jit(solution)/shard_map/ppermute | solution.py:22
  123.5 3.0 %divide_multiply_fusion.4 = f32[8,8,17,64]{3,1,2,0:T(8,128)S(1)} fusion(f32[14,14,3,64]{3,1,2,0:T(8,128)S(1)} %collective-permute-done.17, f32[14,3,16,64]{3,1,2,0:T(4,128)S(1)} %copy.95, f32[3,8,16,64]{3,1,2,0:T(8,128)S(1)} %collective-permute-done.13, f32[8,8,16,64]{3,1,2,0:T(8,128)S(1)} %fusion.48, f32[3,8,16,64]{3,1,2,0:T(8,128)S(1)} %collective-permute-done.12, ...), kind=kLoop, calls=%fused_computation.90 | loop fusion | flops 6266880 | bytes 1386752 | tf_op jit(solution)/shard_map/mul | solution.py:66
  128.1 22.9 %all-to-all-start = ((f32[8,1,8192]{2,1,0:T(1,128)}), f32[8,1,8192]{2,1,0:T(1,128)S(1)}, u32[]{:S(2)}, u32[]{:S(2)}) async-start(f32[8,1,8192]{2,1,0:T(1,128)} %reshape.97), calls=%async_computation | async-start | bytes 524288 | tf_op jit(solution)/shard_map/all_to_all | solution.py:124
  151.0 16.8 %all-to-all-done = f32[8,1,8192]{2,1,0:T(1,128)S(1)} async-done(((f32[8,1,8192]{2,1,0:T(1,128)}), f32[8,1,8192]{2,1,0:T(1,128)S(1)}, u32[]{:S(2)}, u32[]{:S(2)}) %all-to-all-start) | async-done | bytes 262176 | tf_op jit(solution)/shard_map/all_to_all | solution.py:124
  169.9 13.6 %while.27 = (s32[]{:T(128)}, f32[8,1,128,64]{3,2,1,0:T(8,128)S(1)}, f32[8,1,64]{2,0,1:T(8,128)S(1)}, s32[64]{0:T(128)S(1)}, f32[64]{0:T(128)S(1)}, /*index=5*/s32[]{:T(128)}, s32[]{:T(128)}) while((s32[]{:T(128)}, f32[8,1,128,64]{3,2,1,0:T(8,128)S(1)}, f32[8,1,64]{2,0,1:T(8,128)S(1)}, s32[64]{0:T(128)S(1)}, f32[64]{0:T(128)S(1)}, ...), condition=%wide.region_1.2_spmd.clone, body=%wide.region_0.1_spmd.clone.sunk | while | flops 198275 | bytes 1836387 | solution.py:89
  184.1 7.7 %while.26 = (s32[]{:T(128)}, f32[2,512,64]{1,0,2:T(2,128)S(1)}, f32[2,512,64]{1,2,0:T(8,128)S(1)}, bf16[4096,64]{0,1:T(8,128)(2,1)S(1)}, bf16[64,64]{1,0:T(8,128)(2,1)S(1)}, /*index=5*/s32[]{:T(128)}, s32[]{:T(128)}) while((s32[]{:T(128)}, f32[2,512,64]{1,0,2:T(2,128)S(1)}, f32[2,512,64]{1,2,0:T(8,128)S(1)}, bf16[4096,64]{0,1:T(8,128)(2,1)S(1)}, ...), condition=%wide.region_3.4_spmd, body=%wide.region_2.3_spmd.sunk | while | flops 276987904 | bytes 10560609 | solution.py:111
  192.6 24.2 %all_to_all.24 = f32[8,1,8192]{2,1,0:T(1,128)S(1)} all-to-all(f32[8,1,8192]{2,1,0:T(1,128)S(1)} %reshape.99), channel_id=1, replica_groups=mesh['gx'=4,'gy'=16,'gz'=8] {'gz'}, dimensions={0} | all-to-all | bytes 524288 | tf_op jit(solution)/shard_map/all_to_all | solution.py:130
  (213 shorter events, 46.5 us)
Async XLA Ops:
  0.6 33.5 %copy-start.1 = (f32[8,8,16,64]{3,2,1,0:T(8,128)S(1)}, f32[8,8,16,64]{3,2,1,0:T(8,128)}, u32[]{:S(2)}) copy-start(f32[8,8,16,64]{3,2,1,0:T(8,128)} %param.10) | copy-start | bytes 786436
  1.4 5.3 %collective-permute-start = (f32[3,1,8,16]{3,2,1,0:T(8,128)S(1)}, f32[3,1,8,16]{3,2,1,0:T(8,128)S(1)}, u32[]{:S(2)}, u32[]{:S(2)}) collective-permute-start(f32[3,1,8,16]{3,2,1,0:T(8,128)S(1)} %get-tuple-element.257), channel_id=1, source_target_pairs={{0,128},{128,256},{256,384},{1,129},{129,257},{257,385},{2,130},{1... | collective-permute-start | bytes 4616 | tf_op jit(solution)/shard_map/ppermute | solution.py:20
  4.5 4.4 %collective-permute-start.1 = (f32[3,1,8,16]{3,2,1,0:T(8,128)S(1)}, f32[3,1,8,16]{3,2,1,0:T(8,128)S(1)}, u32[]{:S(2)}, u32[]{:S(2)}) collective-permute-start(f32[3,1,8,16]{3,2,1,0:T(8,128)S(1)} %get-tuple-element.256), channel_id=1, source_target_pairs={{128,0},{256,128},{384,256},{129,1},{257,129},{385,257},{130,2},{2... | collective-permute-start | bytes 4616 | tf_op jit(solution)/shard_map/ppermute | solution.py:22
  9.0 6.1 %collective-permute-start.3 = (f32[3,10,1,16]{3,2,1,0:T(1,128)S(1)}, f32[3,10,1,16]{3,2,1,0:T(1,128)S(1)}, u32[]{:S(2)}, u32[]{:S(2)}) collective-permute-start(f32[3,10,1,16]{3,2,1,0:T(1,128)S(1)} %get-tuple-element.255), channel_id=1, source_target_pairs={{8,0},{16,8},{24,16},{32,24},{40,32},{48,40},{56,48},{64,56},{72,6... | collective-permute-start | bytes 5768 | tf_op jit(solution)/shard_map/ppermute | solution.py:22
  13.2 6.6 %collective-permute-start.2 = (f32[3,10,1,16]{3,2,1,0:T(1,128)S(1)}, f32[3,10,1,16]{3,2,1,0:T(1,128)S(1)}, u32[]{:S(2)}, u32[]{:S(2)}) collective-permute-start(f32[3,10,1,16]{3,2,1,0:T(1,128)S(1)} %get-tuple-element.254), channel_id=1, source_target_pairs={{0,8},{8,16},{16,24},{24,32},{32,40},{40,48},{48,56},{56,64},{64,7... | collective-permute-start | bytes 5768 | tf_op jit(solution)/shard_map/ppermute | solution.py:20
  20.0 21.1 %collective-permute-start.5 = (f32[3,10,10,1]{3,2,1,0:T(8,128)S(1)}, f32[3,10,10,1]{3,2,1,0:T(8,128)S(1)}, u32[]{:S(2)}, u32[]{:S(2)}) collective-permute-start(f32[3,10,10,1]{3,2,1,0:T(8,128)S(1)} %get-tuple-element.249), channel_id=1, source_target_pairs={{1,0},{2,1},{3,2},{4,3},{5,4},{6,5},{7,6},{9,8},{10,9},{11,10},{12... | collective-permute-start | bytes 3608 | tf_op jit(solution)/shard_map/ppermute | solution.py:22
  25.4 15.6 %collective-permute-start.4 = (f32[3,10,10,1]{3,2,1,0:T(8,128)S(1)}, f32[3,10,10,1]{3,2,1,0:T(8,128)S(1)}, u32[]{:S(2)}, u32[]{:S(2)}) collective-permute-start(f32[3,10,10,1]{3,2,1,0:T(8,128)S(1)} %get-tuple-element.248), channel_id=1, source_target_pairs={{0,1},{1,2},{2,3},{3,4},{4,5},{5,6},{6,7},{8,9},{9,10},{10,11},{11... | collective-permute-start | bytes 3608 | tf_op jit(solution)/shard_map/ppermute | solution.py:20
  34.3 7.8 %collective-permute-start.6 = (f32[3,8,16,64]{3,1,2,0:T(8,128)S(1)}, f32[3,8,16,64]{3,1,2,0:T(8,128)S(1)}, u32[]{:S(2)}, u32[]{:S(2)}) collective-permute-start(f32[3,8,16,64]{3,1,2,0:T(8,128)S(1)} %copy.114), channel_id=1, source_target_pairs={{0,128},{128,256},{256,384},{1,129},{129,257},{257,385},{2,130},{1... | collective-permute-start | bytes 294920 | tf_op jit(solution)/shard_map/ppermute | solution.py:20
  37.2 6.4 %collective-permute-start.7 = (f32[3,8,16,64]{3,1,2,0:T(8,128)S(1)}, f32[3,8,16,64]{3,1,2,0:T(8,128)S(1)}, u32[]{:S(2)}, u32[]{:S(2)}) collective-permute-start(f32[3,8,16,64]{3,1,2,0:T(8,128)S(1)} %copy.115), channel_id=1, source_target_pairs={{128,0},{256,128},{384,256},{129,1},{257,129},{385,257},{130,2},{2... | collective-permute-start | bytes 294920 | tf_op jit(solution)/shard_map/ppermute | solution.py:22
  43.9 8.0 %collective-permute-start.9 = (f32[14,3,16,64]{3,2,1,0:T(8,128)S(1)}, f32[14,3,16,64]{3,2,1,0:T(8,128)S(1)}, u32[]{:S(2)}, u32[]{:S(2)}) collective-permute-start(f32[14,3,16,64]{3,2,1,0:T(8,128)S(1)} %copy.86), channel_id=1, source_target_pairs={{8,0},{16,8},{24,16},{32,24},{40,32},{48,40},{56,48},{64,56},{72,6... | collective-permute-start | bytes 516104 | tf_op jit(solution)/shard_map/ppermute | solution.py:22
  45.8 10.1 %collective-permute-start.8 = (f32[14,3,16,64]{3,2,1,0:T(8,128)S(1)}, f32[14,3,16,64]{3,2,1,0:T(8,128)S(1)}, u32[]{:S(2)}, u32[]{:S(2)}) collective-permute-start(f32[14,3,16,64]{3,2,1,0:T(8,128)S(1)} %copy.84), channel_id=1, source_target_pairs={{0,8},{8,16},{16,24},{24,32},{32,40},{40,48},{48,56},{56,64},{64,7... | collective-permute-start | bytes 516104 | tf_op jit(solution)/shard_map/ppermute | solution.py:20
  56.3 21.3 %collective-permute-start.11 = (f32[14,14,3,64]{3,1,2,0:T(8,128)S(1)}, f32[14,14,3,64]{3,1,2,0:T(8,128)S(1)}, u32[]{:S(2)}, u32[]{:S(2)}) collective-permute-start(f32[14,14,3,64]{3,1,2,0:T(8,128)S(1)} %get-tuple-element.232), channel_id=1, source_target_pairs={{1,0},{2,1},{3,2},{4,3},{5,4},{6,5},{7,6},{9,8},{10,9},{11,10},{12... | collective-permute-start | bytes 451592 | tf_op jit(solution)/shard_map/ppermute | solution.py:22
  58.2 19.4 %collective-permute-start.10 = (f32[14,14,3,64]{3,1,2,0:T(8,128)S(1)}, f32[14,14,3,64]{3,1,2,0:T(8,128)S(1)}, u32[]{:S(2)}, u32[]{:S(2)}) collective-permute-start(f32[14,14,3,64]{3,1,2,0:T(8,128)S(1)} %get-tuple-element.231), channel_id=1, source_target_pairs={{0,1},{1,2},{2,3},{3,4},{4,5},{5,6},{6,7},{8,9},{9,10},{10,11},{11... | collective-permute-start | bytes 451592 | tf_op jit(solution)/shard_map/ppermute | solution.py:20
  80.7 6.7 %collective-permute-start.13 = (f32[3,8,16,64]{3,1,2,0:T(8,128)S(1)}, f32[3,8,16,64]{3,1,2,0:T(8,128)S(1)}, u32[]{:S(2)}, u32[]{:S(2)}) collective-permute-start(f32[3,8,16,64]{3,1,2,0:T(8,128)S(1)} %get-tuple-element.242), channel_id=1, source_target_pairs={{128,0},{256,128},{384,256},{129,1},{257,129},{385,257},{130,2},{2... | collective-permute-start | bytes 294920 | tf_op jit(solution)/shard_map/ppermute | solution.py:22
  82.6 6.7 %collective-permute-start.12 = (f32[3,8,16,64]{3,1,2,0:T(8,128)S(1)}, f32[3,8,16,64]{3,1,2,0:T(8,128)S(1)}, u32[]{:S(2)}, u32[]{:S(2)}) collective-permute-start(f32[3,8,16,64]{3,1,2,0:T(8,128)S(1)} %get-tuple-element.241), channel_id=1, source_target_pairs={{0,128},{128,256},{256,384},{1,129},{129,257},{257,385},{2,130},{1... | collective-permute-start | bytes 294920 | tf_op jit(solution)/shard_map/ppermute | solution.py:20
  89.7 9.8 %collective-permute-start.15 = (f32[14,3,16,64]{3,2,1,0:T(8,128)S(1)}, f32[14,3,16,64]{3,2,1,0:T(8,128)S(1)}, u32[]{:S(2)}, u32[]{:S(2)}) collective-permute-start(f32[14,3,16,64]{3,2,1,0:T(8,128)S(1)} %copy.94), channel_id=1, source_target_pairs={{8,0},{16,8},{24,16},{32,24},{40,32},{48,40},{56,48},{64,56},{72,6... | collective-permute-start | bytes 516104 | tf_op jit(solution)/shard_map/ppermute | solution.py:22
  91.6 10.1 %collective-permute-start.14 = (f32[14,3,16,64]{3,2,1,0:T(8,128)S(1)}, f32[14,3,16,64]{3,2,1,0:T(8,128)S(1)}, u32[]{:S(2)}, u32[]{:S(2)}) collective-permute-start(f32[14,3,16,64]{3,2,1,0:T(8,128)S(1)} %copy.92), channel_id=1, source_target_pairs={{0,8},{8,16},{16,24},{24,32},{32,40},{40,48},{48,56},{56,64},{64,7... | collective-permute-start | bytes 516104 | tf_op jit(solution)/shard_map/ppermute | solution.py:20
  102.1 21.5 %collective-permute-start.17 = (f32[14,14,3,64]{3,1,2,0:T(8,128)S(1)}, f32[14,14,3,64]{3,1,2,0:T(8,128)S(1)}, u32[]{:S(2)}, u32[]{:S(2)}) collective-permute-start(f32[14,14,3,64]{3,1,2,0:T(8,128)S(1)} %get-tuple-element.230), channel_id=1, source_target_pairs={{1,0},{2,1},{3,2},{4,3},{5,4},{6,5},{7,6},{9,8},{10,9},{11,10},{12... | collective-permute-start | bytes 451592 | tf_op jit(solution)/shard_map/ppermute | solution.py:22
  104.0 19.5 %collective-permute-start.16 = (f32[14,14,3,64]{3,1,2,0:T(8,128)S(1)}, f32[14,14,3,64]{3,1,2,0:T(8,128)S(1)}, u32[]{:S(2)}, u32[]{:S(2)}) collective-permute-start(f32[14,14,3,64]{3,1,2,0:T(8,128)S(1)} %get-tuple-element.229), channel_id=1, source_target_pairs={{0,1},{1,2},{2,3},{3,4},{4,5},{5,6},{6,7},{8,9},{9,10},{10,11},{11... | collective-permute-start | bytes 451592 | tf_op jit(solution)/shard_map/ppermute | solution.py:20
  127.0 42.8 %copy-start.4 = (s32[64]{0:T(128)S(1)}, s32[64]{0:T(128)}, u32[]{:S(2)}) copy-start(s32[64]{0:T(128)} %param.13) | copy-start | bytes 772
  127.0 42.8 %copy-start.5 = (f32[64]{0:T(128)S(1)}, f32[64]{0:T(128)}, u32[]{:S(2)}) copy-start(f32[64]{0:T(128)} %param.12) | copy-start | bytes 772
  128.1 39.7 %all-to-all-start = ((f32[8,1,8192]{2,1,0:T(1,128)}), f32[8,1,8192]{2,1,0:T(1,128)S(1)}, u32[]{:S(2)}, u32[]{:S(2)}) async-start(f32[8,1,8192]{2,1,0:T(1,128)} %reshape.97), calls=%async_computation | async-start | bytes 524288 | tf_op jit(solution)/shard_map/all_to_all | solution.py:124
  169.8 13.9 %copy-start = (bf16[4096,64]{0,1:T(8,128)(2,1)S(1)}, bf16[4096,64]{0,1:T(8,128)(2,1)}, u32[]{:S(2)}) copy-start(bf16[4096,64]{0,1:T(8,128)(2,1)} %param.14) | copy-start | bytes 1572868
  169.9 13.9 %copy-start.2 = (bf16[64,64]{1,0:T(8,128)(2,1)S(1)}, bf16[64,64]{1,0:T(8,128)(2,1)}, u32[]{:S(2)}) copy-start(bf16[64,64]{1,0:T(8,128)(2,1)} %param.15) | copy-start | bytes 24580
  183.5 0.6 copy-start.3
where the time goes:
time: 220 us; the launch traced here: 219 us
  starting transfers between devices  92.7 us (42%)
  waiting for transfers between devices  52.4 us (24%)
  other arithmetic  25.9 us (12%)
  blocking collectives  24.2 us (11%)
  local copies, waits for them, and re-layouts  19.3 us (9%)
    ppermute x9, starting transfers between devices, extended(): lax.ppermute(tail, axis, [(i, (i + 1) % count) for i in range(ends)])  46 us
    all_to_all x1, blocking collectives, per_device(): lax.all_to_all(updated_columns, 'gz', split_axis=2, concat_axis=1, tiled=...  24.2 us
    ppermute x9, starting transfers between devices, extended(): lax.ppermute(head, axis, [((i + 1) % count, i) for i in range(ends)])  23.9 us
    ppermute x9, waiting for transfers between devices, extended(): lax.ppermute(head, axis, [((i + 1) % count, i) for i in range(ends)])  23.1 us
    all_to_all x1, starting transfers between devices, per_device(): lax.all_to_all(advected, 'gz', split_axis=1, concat_axis=2, tiled=True)  22.9 us
    all_to_all x1, waiting for transfers between devices, per_device(): lax.all_to_all(advected, 'gz', split_axis=1, concat_axis=2, tiled=True)  16.8 us
    mul x6, other arithmetic, advect(): face_flux = face_speed[..., None] * estimate  14.1 us
    ppermute x9, waiting for transfers between devices, extended(): lax.ppermute(tail, axis, [(i, (i + 1) % count) for i in range(ends)])  12.6 us
  transfers between devices with their start and end apart: 19, of which 13 were waited for; matrix products, arithmetic and copies ran while one was open for 5% of the time, Pallas kernels for 0%

commit v1 on v0

v1 whole, which is shorter than its diff:
```python
import functools

import jax
import jax.numpy as jnp
from jax import lax
from jax.experimental import pallas as pl
from jax.experimental.pallas import tpu as pltpu
from jax.sharding import PartitionSpec as P

MESH = pl.DeviceIdType.MESH
SUBS = 24
EPS4 = 4e-6
F32 = jnp.float32
BF16 = jnp.bfloat16

OWN = 3 * 32
TOP = 19 * 32
FIELD = 21 * 32
COLUMN = 40 * 8


def weno_line(count, value, speed, emit):
    f_a, f_b, f_c, f_d = value(-3), value(-2), value(-1), value(0)
    d_prev, d_here, d_next = f_b - f_a, f_c - f_b, f_d - f_c
    half_here, half_next = 0.5 * f_c, 0.5 * f_d

    def smooth(e):
        return (13.0 / 3.0) * (e * e) + EPS4

    e_low, e_mid = d_here - d_prev, d_next - d_here
    q_low, q_mid = smooth(e_low), smooth(e_mid)
    t_low = e_mid - e_low
    f_last = f_d
    flux_prev = None
    for face in range(count + 1):
        f_new = value(face + 1)
        d_new = f_new - f_last
        e_high = d_new - d_next
        q_high = smooth(e_high)
        t_high = e_high - e_mid
        g_low = e_low + 2.0 * d_here
        g_mid = d_here + d_next
        g_high = e_high - 2.0 * d_next
        b_low = q_low + g_low * g_low
        b_mid = q_mid + g_mid * g_mid
        b_high = q_high + g_high * g_high
        w_low = b_mid * b_high
        w_mid = b_low * b_high
        w_high = b_low * b_mid
        w_low = w_low * w_low
        w_mid = w_mid * w_mid
        w_high = 0.5 * (w_high * w_high)
        num = w_low * ((1.0 / 3.0) * t_low) + w_high * t_high
        den = w_low + 6.0 * (w_mid + w_high)
        central = (half_here + half_next) - (1.0 / 6.0) * e_mid
        flux = speed(face) * (central - num * pl.reciprocal(den, approx=True))
        if face:
            emit(face - 1, flux - flux_prev)
        flux_prev = flux
        f_last = f_new
        half_here, half_next = half_next, 0.5 * f_new
        d_here, d_next = d_next, d_new
        e_low, e_mid = e_mid, e_high
        q_low, q_mid = q_mid, q_high
        t_low = t_high


def kernel(
    nx, ny, nz,
    mass_ref, courant_ref, rate_ref, steps_ref, gain_ref, collide_ref,
    out_ref, rain_ref,
    raw, gains, field, tend, x_low, x_high, x_out, y_low, y_high, y_out, y_in, winds,
    speed_x, speed_y, speed_z, taps, rain_taps, levels, stage, cells, rounded, pairs, rain,
    load_sem, halo_send, halo_recv, wind_send, wind_recv, sed_send, sed_recv, rain_send, rain_recv,
):
    gx, gy, gz = lax.axis_index("gx"), lax.axis_index("gy"), lax.axis_index("gz")
    odd = lax.rem(gz, 2) == 1

    def when(cond, fn):
        pl.when(cond)(fn)

    sides = [
        (gx > 0, {"gx": lax.rem(gx + nx - 1, nx)}),
        (gx < nx - 1, {"gx": lax.rem(gx + 1, nx)}),
        (gy > 0, {"gy": lax.rem(gy + ny - 1, ny)}),
        (gy < ny - 1, {"gy": lax.rem(gy + 1, ny)}),
        (gz > 0, {"gz": lax.rem(gz + nz - 1, nz)}),
        (gz < nz - 1, {"gz": lax.rem(gz + 1, nz)}),
        (gz > 1, {"gz": lax.rem(gz + nz - 2, nz)}),
        (gz < nz - 2, {"gz": lax.rem(gz + 2, nz)}),
    ]

    barrier = pltpu.get_barrier_semaphore()
    for there, where in sides:
        when(
            there,
            lambda where=where: pl.semaphore_signal(
                barrier, inc=1, device_id=where, device_id_type=MESH
            ),
        )
    mass_load = pltpu.make_async_copy(mass_ref, raw, load_sem.at[0])
    gain_load = pltpu.make_async_copy(gain_ref, gains, load_sem.at[1])
    mass_load.start()
    gain_load.start()

    lane = lax.broadcasted_iota(jnp.int32, (8, 128), 1)
    low = lane < 64

    def turn(v):
        return pltpu.roll(v, 64, 1)

    for d in range(3):
        for y in range(8):
            winds[pl.ds(d * 24 + 8, 8), pl.ds(16 * y, 16)] = courant_ref[d, :, y, :]

    def fill(ref, start, rows):
        ref[pl.ds(start, rows), :] = jnp.zeros((rows, 128), F32)

    def no_x_low():
        fill(x_low, 0, 384)
        fill(winds, 0, 8)

    def no_x_high():
        fill(x_high, 0, 256)
        fill(winds, 16, 8)

    def no_y_low():
        fill(y_in, 0, 384)
        fill(winds, 24, 8)

    def no_y_high():
        fill(y_in, 384, 256)
        fill(winds, 40, 8)

    def no_z_low():
        fill(field, 0, OWN)
        fill(field, FIELD, OWN)
        fill(winds, 48, 8)

    def no_z_high():
        fill(field, TOP, 64)
        fill(field, FIELD + TOP, 64)
        fill(winds, 64, 8)
        for yi in range(4):
            fill(levels, yi * COLUMN + 128, 128)

    for (there, _), fn in zip(
        sides, (no_x_low, no_x_high, no_y_low, no_y_high, no_z_low, no_z_high)
    ):
        when(jnp.logical_not(there), fn)
    def none_above():
        for yi in range(4):
            fill(levels, yi * COLUMN + 256, 64)

    when(gz >= nz - 2, none_above)

    mass_load.wait()

    def pack(z, carry):
        for yi in range(4):
            lo = raw[pl.ds(16 * yi + z, 8, stride=128), :]
            hi = raw[pl.ds(16 * (yi + 4) + z, 8, stride=128), :]
            field[pl.ds(pl.multiple_of(OWN + z * 32 + yi * 8, 8), 8), :] = jnp.concatenate(
                [lo, hi], axis=1
            )
        return carry

    lax.fori_loop(0, 16, pack, 0, unroll=2)

    waits = jnp.int32(0)
    for there, _ in sides:
        waits = waits + there.astype(jnp.int32)
    pl.semaphore_wait(barrier, waits)

    def copy_of(src, dst, send, recv, where):
        return pltpu.make_async_remote_copy(
            src_ref=src, dst_ref=dst, send_sem=send, recv_sem=recv,
            device_id=where, device_id_type=MESH,
        )

    def halos(s):
        base = s * FIELD
        out = []
        spans = [
            (x_out.at[pl.ds(s * 320 + 192, 128)], x_high.at[pl.ds(s * 128, 128)], 0),
            (x_out.at[pl.ds(s * 320, 192)], x_low.at[pl.ds(s * 192, 192)], 1),
            (y_out.at[pl.ds(s * 320 + 192, 128)], y_in.at[pl.ds(384 + s * 128, 128)], 2),
            (y_out.at[pl.ds(s * 320, 192)], y_in.at[pl.ds(s * 192, 192)], 3),
            (field.at[pl.ds(base + OWN, 64)], field.at[pl.ds(base + TOP, 64)], 4),
            (field.at[pl.ds(base + TOP - 96, 96)], field.at[pl.ds(base, 96)], 5),
        ]
        for src, dst, to in spans:
            out.append(
                (to, to ^ 1, copy_of(src, dst, halo_send.at[s, to], halo_recv.at[s, to], sides[to][1]))
            )
        return out

    wind_copies = []
    for d in range(3):
        own = winds.at[pl.ds(d * 24 + 8, 8)]
        for to in (2 * d, 2 * d + 1):
            dst = winds.at[pl.ds(d * 24 + (16 if to == 2 * d else 0), 8)]
            wind_copies.append(
                (to, to ^ 1, copy_of(own, dst, wind_send.at[to], wind_recv.at[to], sides[to][1]))
            )

    def start(copies, only):
        for to, _, copy in copies:
            if to in only:
                when(sides[to][0], copy.start)

    def finish_recv(copies, only):
        for to, source, copy in copies:
            if source in only:
                when(sides[source][0], copy.wait_recv)

    def finish_send(copies):
        for to, _, copy in copies:
            when(sides[to][0], copy.wait_send)

    def pack_x(s):
        base = s * FIELD + OWN
        for k, x in enumerate((5, 6, 7, 0, 1)):
            x_out[pl.ds(s * 320 + k * 64, 64), :] = field[pl.ds(base + x, 64, stride=8), :]

    def pack_y(s):
        base = s * FIELD + OWN

        def body(zi, carry):
            here = base + zi * 32
            for k in range(3):
                lo = field[pl.ds(pl.multiple_of(here + (k + 1) * 8, 8), 8), :]
                hi = field[pl.ds(pl.multiple_of(here + 256 + (k + 1) * 8, 8), 8), :]
                y_out[pl.ds(pl.multiple_of(s * 320 + (zi * 3 + k) * 8, 8), 8), :] = jnp.where(
                    low, turn(lo), hi
                )
            for k in range(2):
                lo = field[pl.ds(pl.multiple_of(here + k * 8, 8), 8), :]
                hi = field[pl.ds(pl.multiple_of(here + 256 + k * 8, 8), 8), :]
                y_out[pl.ds(pl.multiple_of(s * 320 + 192 + (zi * 2 + k) * 8, 8), 8), :] = jnp.where(
                    low, lo, turn(hi)
                )
            return carry

        lax.fori_loop(0, 8, body, 0, unroll=2)

    def send_halos(s):
        copies = halos(s)
        start(copies, (4, 5))
        pack_y(s)
        start(copies, (2, 3))
        pack_x(s)
        start(copies, (0, 1))
        return copies

    def unpack_y(s):
        base = s * FIELD + OWN

        def body(zi, carry):
            here = base + zi * 32
            for k in range(3):
                got = y_in[pl.ds(pl.multiple_of(s * 192 + (zi * 3 + k) * 8, 8), 8), :]
                own_a = turn(field[pl.ds(pl.multiple_of(here + (k + 1) * 8, 8), 8), :])
                own_b = turn(field[pl.ds(pl.multiple_of(here + 256 + (k + 1) * 8, 8), 8), :])
                at = pl.multiple_of((zi * 3 + k) * 8, 8)
                y_low[pl.ds(at, 8), :] = jnp.where(low, got, own_a)
                y_low[pl.ds(at + 192, 8), :] = jnp.where(low, turn(got), own_b)
            for k in range(2):
                got = y_in[pl.ds(pl.multiple_of(384 + s * 128 + (zi * 2 + k) * 8, 8), 8), :]
                own_a = turn(field[pl.ds(pl.multiple_of(here + k * 8, 8), 8), :])
                own_b = turn(field[pl.ds(pl.multiple_of(here + 256 + k * 8, 8), 8), :])
                at = pl.multiple_of((zi * 2 + k) * 8, 8)
                y_high[pl.ds(at, 8), :] = jnp.where(low, own_a, turn(got))
                y_high[pl.ds(at + 128, 8), :] = jnp.where(low, own_b, got)
            return carry

        lax.fori_loop(0, 8, body, 0, unroll=2)

    def pass_x(s):
        base = s * FIELD + OWN

        def body(p, carry):
            at = pl.multiple_of(p * 16, 16)

            def value(i):
                if i < 0:
                    return x_low[pl.ds(s * 192 + (i + 3) * 64 + at, 16), :]
                if i > 7:
                    return x_high[pl.ds(s * 128 + (i - 8) * 64 + at, 16), :]
                return field[pl.ds(base + p * 128 + i, 16, stride=8), :]

            def speed(k):
                return speed_x[pl.ds(k * 64 + at, 16), :]

            def emit(i, change):
                tend[pl.ds(p * 128 + i, 16, stride=8), :] = -change

            weno_line(8, value, speed, emit)
            return carry

        lax.fori_loop(0, 4, body, 0)

    def pass_y(s):
        base = s * FIELD + OWN

        def body(z, carry):
            def value(i):
                if i < 0:
                    return y_low[pl.ds(pl.multiple_of((z * 3 + i + 3) * 8, 8), 8), :]
                if i > 3:
                    return y_high[pl.ds(pl.multiple_of((z * 2 + i - 4) * 8, 8), 8), :]
                return field[pl.ds(pl.multiple_of(base + z * 32 + i * 8, 8), 8), :]

            def speed(k):
                return speed_y[pl.ds(pl.multiple_of((z * 5 + k) * 8, 8), 8), :]

            def emit(i, change):
                at = pl.ds(pl.multiple_of(z * 32 + i * 8, 8), 8)
                tend[at, :] = tend[at, :] - change

            weno_line(4, value, speed, emit)
            return carry

        lax.fori_loop(0, 16, body, 0, unroll=2)

    def pass_z(s, p):
        at = pl.multiple_of(p * 16, 16)

        def value(i):
            return field[pl.ds(s * FIELD + (i + 3) * 32 + at, 16), :]

        def speed(k):
            return speed_z[pl.ds(k * 32 + at, 16), :]

        def emit(i, change):
            stepped = value(i) + (tend[pl.ds(i * 32 + at, 16), :] - change)
            if s == 0:
                field[pl.ds(FIELD + OWN + i * 32 + at, 16), :] = stepped
            else:
                before = field[pl.ds(OWN + i * 32 + at, 16), :]
                settled = 0.5 * before + 0.5 * stepped
                for k in range(2):
                    levels[pl.ds((2 * p + k) * COLUMN + i * 8, 8), :] = settled[8 * k : 8 * k + 8]

        weno_line(16, value, speed, emit)

    start(wind_copies, (4, 5))
    first = send_halos(0)
    start(wind_copies, (0, 1, 2, 3))

    rates = jnp.concatenate([rate_ref[...], rate_ref[...]], axis=1)
    counts = jnp.concatenate([steps_ref[...], steps_ref[...]], axis=1)
    tap = (lax.broadcasted_iota(jnp.int32, (32, 128), 0) == 0).astype(F32)
    fallen = jnp.zeros((32, 128), F32)
    for s in range(SUBS):
        rate = jnp.where(s < counts, rates, 0.0)
        fallen = fallen + rate * tap
        tap = tap + rate * (pltpu.roll(tap, 1, 0) - tap)
    taps[...] = tap
    rain_taps[...] = fallen

    column = jnp.where(low, 0, 64)

    def spread(v, index):
        return jnp.take_along_axis(v, index, axis=1)

    def speeds_x():
        right = 0.5 * (winds[pl.ds(8, 8), :] + winds[pl.ds(9, 8), :])
        left = jnp.broadcast_to(0.5 * (winds[pl.ds(7, 1), :] + winds[pl.ds(8, 1), :]), (8, 128))

        def body(z, carry):
            for yi in range(4):
                index = column + (16 * yi + z)
                row = z * 4 + yi
                speed_x[pl.ds(64 + row, 8, stride=64), :] = spread(right, index)
                speed_x[pl.ds(row, 1), :] = spread(left, index)[0:1, :]
            return carry

        lax.fori_loop(0, 16, body, 0, unroll=2)

    def speeds_y():
        own, before, after = (winds[pl.ds(24 + k, 8), :] for k in (8, 0, 16))
        following = jnp.where(lane < 112, pltpu.roll(own, 112, 1), pltpu.roll(after, 112, 1))
        right = 0.5 * (own + following)
        left = 0.5 * (own + pltpu.roll(before, 16, 1))

        def body(z, carry):
            first_face = jnp.where(
                low,
                spread(left, jnp.zeros_like(lane) + z),
                spread(right, jnp.zeros_like(lane) + (48 + z)),
            )
            speed_y[pl.ds(pl.multiple_of(z * 40, 8), 8), :] = first_face
            for k in range(1, 5):
                speed_y[pl.ds(pl.multiple_of(z * 40 + k * 8, 8), 8), :] = spread(
                    right, column + (16 * (k - 1) + z)
                )
            return carry

        lax.fori_loop(0, 16, body, 0, unroll=2)

    def speeds_z():
        own, before, after = (winds[pl.ds(48 + k, 8), :] for k in (8, 0, 16))
        following = jnp.where(
            lax.rem(lane, 16) == 15, pltpu.roll(after, 15, 1), pltpu.roll(own, 127, 1)
        )
        right = 0.5 * (own + following)
        left = 0.5 * (own + pltpu.roll(before, 113, 1))
        for yi in range(4):
            speed_z[pl.ds(yi * 8, 8), :] = spread(left, column + 16 * yi)

        def body(z, carry):
            for yi in range(4):
                speed_z[pl.ds(pl.multiple_of(32 + z * 32 + yi * 8, 8), 8), :] = spread(
                    right, column + (16 * yi + z)
                )
            return carry

        lax.fori_loop(0, 16, body, 0, unroll=2)

    finish_recv(wind_copies, (0, 1))
    speeds_x()
    finish_recv(first, (0, 1))
    pass_x(0)
    finish_recv(wind_copies, (2, 3))
    speeds_y()
    finish_recv(first, (2, 3))
    unpack_y(0)
    pass_y(0)
    finish_recv(wind_copies, (4, 5))
    speeds_z()
    finish_recv(first, (4, 5))
    for p in range(2):
        pass_z(0, p)

    second = send_halos(1)
    finish_recv(second, (0, 1))
    pass_x(1)
    finish_recv(second, (2, 3))
    unpack_y(1)
    pass_y(1)
    finish_recv(second, (4, 5))

    def sed_copy(kind, yi):
        source, target, side = ((0, 16, 4), (8, 24, 4), (0, 32, 6), (16, 32, 4))[kind]
        return copy_of(
            levels.at[pl.ds(yi * COLUMN + source * 8, 64)],
            levels.at[pl.ds(yi * COLUMN + target * 8, 64)],
            sed_send.at[yi, kind], sed_recv.at[yi, min(kind, 2)], sides[side][1],
        )

    above = gz < nz - 1
    above_two = gz < nz - 2
    sends = (gz > 0, gz > 0, jnp.logical_and(odd, gz > 1), jnp.logical_and(odd, above))

    def sed_start(kind, yi):
        when(sends[kind], sed_copy(kind, yi).start)

    for p in range(2):
        pass_z(1, p)
        for yi in (2 * p, 2 * p + 1):
            sed_start(0, yi)
    for yi in range(4):
        sed_start(1, yi)
        sed_start(2, yi)
    for yi in range(4):
        when(above, sed_copy(0, yi).wait_recv)
        sed_start(3, yi)

    def rain_copy(step):
        side = sides[5] if step == 0 else sides[7]
        return copy_of(rain, rain, rain_send.at[step], rain_recv.at[0], side[1])

    def rain_pass():
        rain_copy(0).start()
        when(above_two, rain_copy(1).start)

    def rain_make():
        def body(yi, carry):
            total = jnp.zeros((8, 128), F32)
            for m in range(SUBS):
                at = pl.ds(pl.multiple_of(yi * COLUMN + m * 8, 8), 8)
                total = total + rain_taps[pl.ds(m, 1), :] * levels[at, :]
            rain[pl.ds(pl.multiple_of(yi * 8, 8), 8), :] = total
            return carry

        lax.fori_loop(0, 4, body, 0)
        rain_pass()

    when(gz == 0, rain_make)

    def rain_forward():
        rain_copy(0).wait_recv()
        rain_pass()

    gain_load.wait()

    def settle(yi, carry):
        def body(group, inner):
            base = yi * COLUMN + group * 64
            sums = [None] * 8
            for j in range(8 + SUBS):
                v = levels[pl.ds(pl.multiple_of(base + j * 8, 8), 8), :]
                for k in range(8):
                    if 0 <= j - k <= SUBS:
                        term = taps[pl.ds(j - k, 1), :] * v
                        sums[k] = term if sums[k] is None else sums[k] + term
            for k in range(8):
                stage[pl.ds(pl.multiple_of(group * 64 + k * 8, 8), 8), :] = sums[k]
            return inner

        lax.fori_loop(0, 2, body, 0)
        return carry

    def breakup(yi):
        block = jnp.concatenate([stage[pl.ds(x, 16, stride=8), :] for x in range(8)], axis=0).T
        for h in range(2):
            cells[:, 128 * h : 128 * h + 128] = block[64 * h : 64 * h + 64]
        small = cells[...].astype(BF16)
        rounded[...] = small.astype(F32)

        def body(i, carry):
            term = rounded[pl.ds(i, 1), :] * rounded[...]
            pairs[pl.ds(pl.multiple_of(i * 64, 64), 64), :] = term.astype(BF16)
            return carry

        lax.fori_loop(0, 64, body, 0, unroll=4)
        gained = jnp.dot(gains[...], pairs[...], preferred_element_type=F32)
        loss = lax.dot_general(
            collide_ref[...], small, (((0,), (0,)), ((), ())), preferred_element_type=F32
        )
        settled = cells[...]
        result = settled + gained - settled * loss
        for h in range(2):
            back = result[:, 128 * h : 128 * h + 128].T
            out_ref[:, 4 * h + yi] = back.reshape(8, 16, 64)

    for yi in range(4):
        when(above, sed_copy(1, yi).wait_recv)
        when(above_two, sed_copy(2, yi).wait_recv)
        settle(yi, 0)
        breakup(yi)
        if yi < 3:
            when(gz == 2 * yi + 2, rain_forward)

    when(odd, rain_copy(0).wait_recv)
    mine = rain[pl.ds(pl.multiple_of(lax.rem(gz, 4) * 8, 8), 8), :]
    upper = (jnp.zeros((8, 128), jnp.int32) + gz) >= 4
    rain_ref[:, 0, :] = jnp.where(upper, turn(mine), mine)[:, :64]

    when(jnp.logical_not(odd), rain_copy(0).wait_send)
    when(jnp.logical_and(jnp.logical_not(odd), above_two), rain_copy(1).wait_send)
    for yi in range(4):
        for kind in range(4):
            when(sends[kind], sed_copy(kind, yi).wait_send)
    finish_send(wind_copies)
    finish_send(first)
    finish_send(second)


def per_device(sizes, bin_mass, courant, sub_courant, fall_steps, frag_gain, collide):
    vmem, dma = pltpu.VMEM, pltpu.SemaphoreType.DMA
    out, rain = pl.pallas_call(
        functools.partial(kernel, *sizes),
        out_shape=(
            jax.ShapeDtypeStruct((8, 8, 16, 64), F32),
            jax.ShapeDtypeStruct((8, 1, 64), F32),
        ),
        in_specs=[
            pl.BlockSpec(memory_space=pl.ANY),
            pl.BlockSpec(memory_space=vmem),
            pl.BlockSpec(memory_space=vmem),
            pl.BlockSpec(memory_space=vmem),
            pl.BlockSpec(memory_space=pl.ANY),
            pl.BlockSpec(memory_space=vmem),
        ],
        out_specs=(pl.BlockSpec(memory_space=vmem), pl.BlockSpec(memory_space=vmem)),
        scratch_shapes=[
            vmem((1024, 64), F32),
            vmem((64, 4096), BF16),
            vmem((2 * FIELD, 128), F32),
            vmem((512, 128), F32),
            vmem((384, 128), F32),
            vmem((256, 128), F32),
            vmem((640, 128), F32),
            vmem((384, 128), F32),
            vmem((256, 128), F32),
            vmem((640, 128), F32),
            vmem((640, 128), F32),
            vmem((72, 128), F32),
            vmem((9 * 64, 128), F32),
            vmem((16 * 40, 128), F32),
            vmem((17 * 32, 128), F32),
            vmem((32, 128), F32),
            vmem((32, 128), F32),
            vmem((4 * COLUMN, 128), F32),
            vmem((128, 128), F32),
            vmem((64, 256), F32),
            vmem((64, 256), F32),
            vmem((4096, 256), BF16),
            vmem((32, 128), F32),
            dma((2,)),
            dma((2, 6)),
            dma((2, 6)),
            dma((6,)),
            dma((6,)),
            dma((4, 4)),
            dma((4, 3)),
            dma((2,)),
            dma((1,)),
        ],
        compiler_params=pltpu.CompilerParams(
            collective_id=0, has_side_effects=True, vmem_limit_bytes=40 << 20
        ),
    )(
        bin_mass.reshape(1024, 64),
        courant,
        sub_courant.reshape(1, 64),
        fall_steps.reshape(1, 64),
        frag_gain.T,
        collide,
    )
    return out, rain


def solution(mesh):
    in_specs = (P("gx", "gy", "gz", None), P(None, "gx", "gy", "gz"), P(), P(), P(), P())
    out_specs = (P("gx", "gy", "gz", None), P("gx", ("gy", "gz"), None))
    sizes = tuple(mesh.shape[a] for a in ("gx", "gy", "gz"))
    return jax.shard_map(
        functools.partial(per_device, sizes),
        mesh=mesh,
        in_specs=in_specs,
        out_specs=out_specs,
        check_vma=False,
    )
```

time: 220 us -> 59.9 us (0.27)
  the two profiles are of different devices: /device:TPU:67 before, /device:TPU:25 now
where the time goes in v1:
time: 59.9 us; the launch traced here: 59.6 us
  Pallas kernels  53.2 us (89%)
  local copies, waits for them, and re-layouts  5.73 us (10%)
  between operations  0.66 us (1%)
    pallas_call x1, Pallas kernels, per_device(): pl.pallas_call(functools.partial(kernel, *sizes), out_shape=(jax.ShapeDty...  53.2 us
    unnamed x14, local copies, waits for them, and re-layouts  5.73 us

profile of v1, /device:TPU:25, one launch (start us, length us, event | category | flops | bytes accessed | tf_op | source)
XLA Modules:
  0.0 59.6 jit_solution(2935405370910801867)
XLA Ops:
  0.6 0.0 copy-start.4
  0.6 0.0 copy-start.5
  0.7 0.6 %copy-done.4 = f32[64]{0:T(128)S(1)} copy-done((f32[64]{0:T(128)S(1)}, f32[64]{0:T(128)}, u32[]{:S(2)}) %copy-start.4) | copy-done | bytes 280
  1.3 0.0 copy-done.5
  1.3 0.0 copy-start
  1.3 1.0 %copy-done = f32[8,8,16,64]{3,2,1,0:T(8,128)S(1)} copy-done((f32[8,8,16,64]{3,2,1,0:T(8,128)S(1)}, f32[8,8,16,64]{3,2,1,0:T(8,128)}, u32[]{:S(2)}) %copy-start) | copy-done | bytes 262168
  2.3 0.0 copy-start.1
  2.3 1.0 %copy-done.1 = bf16[4096,64]{0,1:T(8,128)(2,1)S(1)} copy-done((bf16[4096,64]{0,1:T(8,128)(2,1)S(1)}, bf16[4096,64]{0,1:T(8,128)(2,1)}, u32[]{:S(2)}) %copy-start.1) | copy-done | bytes 524312
  3.4 0.0 copy-start.2
  3.4 0.9 %copy-done.2 = f32[3,8,8,16]{3,2,1,0:T(8,128)S(1)} copy-done((f32[3,8,8,16]{3,2,1,0:T(8,128)S(1)}, f32[3,8,8,16]{3,2,1,0:T(8,128)}, u32[]{:S(2)}) %copy-start.2) | copy-done | bytes 12312
  4.3 0.0 copy-start.3
  4.3 0.7 %copy-done.3 = bf16[64,64]{1,0:T(8,128)(2,1)S(1)} copy-done((bf16[64,64]{1,0:T(8,128)(2,1)S(1)}, bf16[64,64]{1,0:T(8,128)(2,1)}, u32[]{:S(2)}) %copy-start.3) | copy-done | bytes 8216
  5.0 53.2 %shard_map.77 = (f32[8,8,16,64]{3,2,1,0:T(8,128)S(1)}, f32[8,1,64]{2,1,0:T(1,128)S(1)}) custom-call(f32[1024,64]{1,0:T(8,128)S(1)} %bitcast.4, f32[3,8,8,16]{3,2,1,0:T(8,128)S(1)} %copy-done.2, f32[1,64]{1,0:T(1,128)S(1)} %bitcast.6, s32[1,64]{1,0:T(1,128)S(1)} %bitcast.7, bf16[64,4096]{1,0:T(8,128)(2,1)S(1)} %bitcast.5, bf16[64,64]{1,0:T(8,128)(2,1)S(1)} %copy-done.3), custom_call_target="tpu_custom_call" | custom-call | tf_op jit(solution)/shard_map/pallas_call | solution.py:563
  58.2 0.8 %copy.10 = f32[8,8,16,64]{3,2,1,0:T(8,128)} copy(f32[8,8,16,64]{3,2,1,0:T(8,128)S(1)} %get-tuple-element.4) | data formatting | bytes 524288
  59.0 0.6 copy.11
Async XLA Ops:
  0.6 0.7 %copy-start.4 = (f32[64]{0:T(128)S(1)}, f32[64]{0:T(128)}, u32[]{:S(2)}) copy-start(f32[64]{0:T(128)} %param.8) | copy-start | bytes 772
  0.6 0.7 %copy-start.5 = (s32[64]{0:T(128)S(1)}, s32[64]{0:T(128)}, u32[]{:S(2)}) copy-start(s32[64]{0:T(128)} %param.9) | copy-start | bytes 772
  1.3 1.0 %copy-start = (f32[8,8,16,64]{3,2,1,0:T(8,128)S(1)}, f32[8,8,16,64]{3,2,1,0:T(8,128)}, u32[]{:S(2)}) copy-start(f32[8,8,16,64]{3,2,1,0:T(8,128)} %param.6) | copy-start | bytes 786436
  2.3 1.0 %copy-start.1 = (bf16[4096,64]{0,1:T(8,128)(2,1)S(1)}, bf16[4096,64]{0,1:T(8,128)(2,1)}, u32[]{:S(2)}) copy-start(bf16[4096,64]{0,1:T(8,128)(2,1)} %param.10) | copy-start | bytes 1572868
  3.4 0.9 %copy-start.2 = (f32[3,8,8,16]{3,2,1,0:T(8,128)S(1)}, f32[3,8,8,16]{3,2,1,0:T(8,128)}, u32[]{:S(2)}) copy-start(f32[3,8,8,16]{3,2,1,0:T(8,128)} %courant_ref.1) | copy-start | bytes 36868
  4.3 0.7 %copy-start.3 = (bf16[64,64]{1,0:T(8,128)(2,1)S(1)}, bf16[64,64]{1,0:T(8,128)(2,1)}, u32[]{:S(2)}) copy-start(bf16[64,64]{1,0:T(8,128)(2,1)} %collide_ref.1) | copy-start | bytes 24580

commit v2 on v1

v2 whole, which is shorter than its diff:
```python
import functools

import jax
import jax.numpy as jnp
from jax import lax
from jax.experimental import pallas as pl
from jax.experimental.pallas import tpu as pltpu
from jax.sharding import PartitionSpec as P

MESH = pl.DeviceIdType.MESH
SUBS = 24
EPS4 = 4e-6
F32 = jnp.float32
BF16 = jnp.bfloat16

OWN = 3 * 32
TOP = 19 * 32
FIELD = 21 * 32
COLUMN = 40 * 8


def weno_line(count, value, speed, emit):
    f_a, f_b, f_c, f_d = value(-3), value(-2), value(-1), value(0)
    d_prev, d_here, d_next = f_b - f_a, f_c - f_b, f_d - f_c
    half_here, half_next = 0.5 * f_c, 0.5 * f_d

    def smooth(e):
        return (13.0 / 3.0) * (e * e) + EPS4

    e_low, e_mid = d_here - d_prev, d_next - d_here
    q_low, q_mid = smooth(e_low), smooth(e_mid)
    t_low = e_mid - e_low
    f_last = f_d
    flux_prev = None
    for face in range(count + 1):
        f_new = value(face + 1)
        d_new = f_new - f_last
        e_high = d_new - d_next
        q_high = smooth(e_high)
        t_high = e_high - e_mid
        g_low = e_low + 2.0 * d_here
        g_mid = d_here + d_next
        g_high = e_high - 2.0 * d_next
        b_low = q_low + g_low * g_low
        b_mid = q_mid + g_mid * g_mid
        b_high = q_high + g_high * g_high
        w_low = b_mid * b_high
        w_mid = b_low * b_high
        w_high = b_low * b_mid
        w_low = w_low * w_low
        w_mid = w_mid * w_mid
        w_high = 0.5 * (w_high * w_high)
        num = w_low * ((1.0 / 3.0) * t_low) + w_high * t_high
        den = w_low + 6.0 * (w_mid + w_high)
        central = (half_here + half_next) - (1.0 / 6.0) * e_mid
        flux = speed(face) * (central - num * pl.reciprocal(den, approx=True))
        if face:
            emit(face - 1, flux - flux_prev)
        flux_prev = flux
        f_last = f_new
        half_here, half_next = half_next, 0.5 * f_new
        d_here, d_next = d_next, d_new
        e_low, e_mid = e_mid, e_high
        q_low, q_mid = q_mid, q_high
        t_low = t_high


def kernel(
    nx, ny, nz,
    mass_hbm, courant_hbm, rate_hbm, steps_hbm, gain_hbm, collide_hbm,
    out_ref, rain_ref,
    raw, courant_ref, rate_ref, steps_ref, gains, collide_ref, field, tend, x_low, x_high, x_out, y_low, y_high, y_out, y_in, winds,
    speed_x, speed_y, speed_z, taps, rain_taps, levels, stage, cells, rounded, rain,
    load_sem, halo_send, halo_recv, wind_send, wind_recv, sed_send, sed_recv, rain_send, rain_recv,
):
    gx, gy, gz = lax.axis_index("gx"), lax.axis_index("gy"), lax.axis_index("gz")
    parity = lax.rem(gz, 2)
    odd = parity == 1
    even = parity == 0
    near_half, far_half = 1 - parity, parity

    def when(cond, fn):
        pl.when(cond)(fn)

    sides = [
        (gx > 0, {"gx": lax.rem(gx + nx - 1, nx)}),
        (gx < nx - 1, {"gx": lax.rem(gx + 1, nx)}),
        (gy > 0, {"gy": lax.rem(gy + ny - 1, ny)}),
        (gy < ny - 1, {"gy": lax.rem(gy + 1, ny)}),
        (gz > 0, {"gz": lax.rem(gz + nz - 1, nz)}),
        (gz < nz - 1, {"gz": lax.rem(gz + 1, nz)}),
    ]

    barrier = pltpu.get_barrier_semaphore()
    for there, where in sides:
        when(
            there,
            lambda where=where: pl.semaphore_signal(
                barrier, inc=1, device_id=where, device_id_type=MESH
            ),
        )
    loads = [
        pltpu.make_async_copy(source, target, load_sem.at[k])
        for k, (source, target) in enumerate(
            (
                (mass_hbm, raw),
                (courant_hbm, courant_ref),
                (rate_hbm, rate_ref),
                (steps_hbm, steps_ref),
                (gain_hbm, gains),
                (collide_hbm, collide_ref),
            )
        )
    ]
    for load in loads:
        load.start()

    lane = lax.broadcasted_iota(jnp.int32, (8, 128), 1)
    low = lane < 64

    def turn(v):
        return pltpu.roll(v, 64, 1)

    def fill(ref, start, rows):
        ref[pl.ds(start, rows), :] = jnp.zeros((rows, 128), F32)

    def no_x_low():
        fill(x_low, 0, 384)
        fill(winds, 0, 8)

    def no_x_high():
        fill(x_high, 0, 256)
        fill(winds, 16, 8)

    def no_y_low():
        fill(y_in, 0, 384)
        fill(winds, 24, 8)

    def no_y_high():
        fill(y_in, 384, 256)
        fill(winds, 40, 8)

    def no_z_low():
        fill(field, 0, OWN)
        fill(field, FIELD, OWN)
        fill(winds, 48, 8)

    def no_z_high():
        fill(field, TOP, 64)
        fill(field, FIELD + TOP, 64)
        fill(winds, 64, 8)
        for yi in range(4):
            fill(levels, yi * COLUMN + 128, 128)

    for (there, _), fn in zip(
        sides, (no_x_low, no_x_high, no_y_low, no_y_high, no_z_low, no_z_high)
    ):
        when(jnp.logical_not(there), fn)
    def none_above():
        for yi in range(4):
            fill(levels, yi * COLUMN + 256, 64)

    when(gz >= nz - 2, none_above)

    loads[0].wait()

    def pack(z, carry):
        for yi in range(4):
            lo = raw[pl.ds(16 * yi + z, 8, stride=128), :]
            hi = raw[pl.ds(16 * (yi + 4) + z, 8, stride=128), :]
            field[pl.ds(pl.multiple_of(OWN + z * 32 + yi * 8, 8), 8), :] = jnp.concatenate(
                [lo, hi], axis=1
            )
        return carry

    lax.fori_loop(0, 16, pack, 0, unroll=2)

    loads[1].wait()
    for d in range(3):
        for y in range(8):
            winds[pl.ds(d * 24 + 8, 8), pl.ds(16 * y, 16)] = courant_ref[d, :, y, :]

    waits = jnp.int32(0)
    for there, _ in sides:
        waits = waits + there.astype(jnp.int32)
    pl.semaphore_wait(barrier, waits)

    def copy_of(src, dst, send, recv, where):
        return pltpu.make_async_remote_copy(
            src_ref=src, dst_ref=dst, send_sem=send, recv_sem=recv,
            device_id=where, device_id_type=MESH,
        )

    def halo(s, slot, to, src, dst):
        return (
            to,
            to ^ 1,
            copy_of(src, dst, halo_send.at[slot, to], halo_recv.at[slot, to], sides[to][1]),
        )

    def halos_xy(s, slot, half, halves):
        def at(start, rows):
            return pl.ds(pl.multiple_of(start + half * rows, 8), rows * halves)

        return [
            halo(s, slot, 0, x_out.at[at(s * 320 + 192, 64)], x_high.at[at(s * 128, 64)]),
            halo(s, slot, 1, x_out.at[at(s * 320, 96)], x_low.at[at(s * 192, 96)]),
            halo(s, slot, 2, y_out.at[at(s * 320 + 192, 64)], y_in.at[at(384 + s * 128, 64)]),
            halo(s, slot, 3, y_out.at[at(s * 320, 96)], y_in.at[at(s * 192, 96)]),
        ]

    def halos_z(s):
        base = s * FIELD
        return [
            halo(s, s, 4, field.at[pl.ds(base + OWN, 64)], field.at[pl.ds(base + TOP, 64)]),
            halo(s, s, 5, field.at[pl.ds(base + TOP - 96, 96)], field.at[pl.ds(base, 96)]),
        ]

    wind_copies = []
    for d in range(3):
        own = winds.at[pl.ds(d * 24 + 8, 8)]
        for to in (2 * d, 2 * d + 1):
            dst = winds.at[pl.ds(d * 24 + (16 if to == 2 * d else 0), 8)]
            wind_copies.append(
                (to, to ^ 1, copy_of(own, dst, wind_send.at[to], wind_recv.at[to], sides[to][1]))
            )

    def start(copies, only):
        for to, _, copy in copies:
            if to in only:
                when(sides[to][0], copy.start)

    def finish_recv(copies, only):
        for to, source, copy in copies:
            if source in only:
                when(sides[source][0], copy.wait_recv)

    def finish_send(copies):
        for to, _, copy in copies:
            when(sides[to][0], copy.wait_send)

    def by_parity(even_side, fn):
        when(even, lambda: fn((even_side,)))
        when(odd, lambda: fn((9 - even_side,)))

    def start_near(copies):
        by_parity(5, lambda only: start(copies, only))

    def start_far(copies):
        by_parity(4, lambda only: start(copies, only))

    def recv_near(copies):
        by_parity(5, lambda only: finish_recv(copies, only))

    def recv_far(copies):
        by_parity(4, lambda only: finish_recv(copies, only))

    def pack_x(s, half):
        base = s * FIELD + OWN + half * 256
        for k in range(3):
            x_out[pl.ds(pl.multiple_of(s * 320 + half * 96 + k * 32, 8), 32), :] = field[
                pl.ds(base + 5 + k, 32, stride=8), :
            ]
        for k in range(2):
            x_out[pl.ds(pl.multiple_of(s * 320 + 192 + half * 64 + k * 32, 8), 32), :] = field[
                pl.ds(base + k, 32, stride=8), :
            ]

    def pack_y(s, half):
        base = s * FIELD + OWN + half * 256
        for zi in range(4):
            here = base + zi * 32
            for k in range(3):
                lo = field[pl.ds(pl.multiple_of(here + (k + 1) * 8, 8), 8), :]
                hi = field[pl.ds(pl.multiple_of(here + 128 + (k + 1) * 8, 8), 8), :]
                at = s * 320 + half * 96 + (zi * 3 + k) * 8
                y_out[pl.ds(pl.multiple_of(at, 8), 8), :] = jnp.where(low, turn(lo), hi)
            for k in range(2):
                lo = field[pl.ds(pl.multiple_of(here + k * 8, 8), 8), :]
                hi = field[pl.ds(pl.multiple_of(here + 128 + k * 8, 8), 8), :]
                at = s * 320 + 192 + half * 64 + (zi * 2 + k) * 8
                y_out[pl.ds(pl.multiple_of(at, 8), 8), :] = jnp.where(low, lo, turn(hi))

    def unpack_y(s, half):
        base = s * FIELD + OWN + half * 256
        for zi in range(4):
            here = base + zi * 32
            for k in range(3):
                at = half * 96 + (zi * 3 + k) * 8
                got = y_in[pl.ds(pl.multiple_of(s * 192 + at, 8), 8), :]
                own_a = turn(field[pl.ds(pl.multiple_of(here + (k + 1) * 8, 8), 8), :])
                own_b = turn(field[pl.ds(pl.multiple_of(here + 128 + (k + 1) * 8, 8), 8), :])
                at = half * 192 + (zi * 3 + k) * 8
                y_low[pl.ds(pl.multiple_of(at, 8), 8), :] = jnp.where(low, got, own_a)
                y_low[pl.ds(pl.multiple_of(at + 96, 8), 8), :] = jnp.where(low, turn(got), own_b)
            for k in range(2):
                at = 384 + s * 128 + half * 64 + (zi * 2 + k) * 8
                got = y_in[pl.ds(pl.multiple_of(at, 8), 8), :]
                own_a = turn(field[pl.ds(pl.multiple_of(here + k * 8, 8), 8), :])
                own_b = turn(field[pl.ds(pl.multiple_of(here + 128 + k * 8, 8), 8), :])
                at = half * 128 + (zi * 2 + k) * 8
                y_high[pl.ds(pl.multiple_of(at, 8), 8), :] = jnp.where(low, own_a, turn(got))
                y_high[pl.ds(pl.multiple_of(at + 64, 8), 8), :] = jnp.where(low, own_b, got)

    def pass_x(s, half):
        base = s * FIELD + OWN

        def body(q, carry):
            at = half * 32 + q * 16

            def value(i):
                if i < 0:
                    row = s * 192 + half * 96 + (i + 3) * 32 + q * 16
                    return x_low[pl.ds(pl.multiple_of(row, 8), 16), :]
                if i > 7:
                    row = s * 128 + half * 64 + (i - 8) * 32 + q * 16
                    return x_high[pl.ds(pl.multiple_of(row, 8), 16), :]
                return field[pl.ds(base + at * 8 + i, 16, stride=8), :]

            def speed(k):
                return speed_x[pl.ds(pl.multiple_of(k * 64 + at, 8), 16), :]

            def emit(i, change):
                tend[pl.ds(at * 8 + i, 16, stride=8), :] = -change

            weno_line(8, value, speed, emit)
            return carry

        lax.fori_loop(0, 2, body, 0)

    def pass_y(s, half):
        base = s * FIELD + OWN

        def body(zi, carry):
            z = half * 8 + zi

            def value(i):
                if i < 0:
                    return y_low[pl.ds(pl.multiple_of((z * 3 + i + 3) * 8, 8), 8), :]
                if i > 3:
                    return y_high[pl.ds(pl.multiple_of((z * 2 + i - 4) * 8, 8), 8), :]
                return field[pl.ds(pl.multiple_of(base + z * 32 + i * 8, 8), 8), :]

            def speed(k):
                return speed_y[pl.ds(pl.multiple_of((z * 5 + k) * 8, 8), 8), :]

            def emit(i, change):
                at = pl.ds(pl.multiple_of(z * 32 + i * 8, 8), 8)
                tend[at, :] = tend[at, :] - change

            weno_line(4, value, speed, emit)
            return carry

        lax.fori_loop(0, 8, body, 0, unroll=2)

    def pass_z(s, first_level, count):
        for p in range(2):
            at = first_level * 32 + p * 16

            def value(i):
                return field[pl.ds(pl.multiple_of(s * FIELD + (i + 3) * 32 + at, 8), 16), :]

            def speed(k):
                return speed_z[pl.ds(pl.multiple_of(k * 32 + at, 8), 16), :]

            def emit(i, change):
                row = i * 32 + at
                stepped = value(i) + (tend[pl.ds(pl.multiple_of(row, 8), 16), :] - change)
                if s == 0:
                    field[pl.ds(pl.multiple_of(FIELD + OWN + row, 8), 16), :] = stepped
                else:
                    before = field[pl.ds(pl.multiple_of(OWN + row, 8), 16), :]
                    settled = 0.5 * before + 0.5 * stepped
                    for k in range(2):
                        to = (2 * p + k) * COLUMN + (first_level + i) * 8
                        levels[pl.ds(pl.multiple_of(to, 8), 8), :] = settled[8 * k : 8 * k + 8]

            weno_line(count, value, speed, emit)

    first_z, first_xy = halos_z(0), halos_xy(0, 0, 0, 2)
    start_far(first_z)
    start_far(wind_copies)
    start_near(first_z)
    start_near(wind_copies)
    start(wind_copies, (0, 1, 2, 3))
    for half in range(2):
        pack_y(0, half)
    start(first_xy, (2, 3))
    for half in range(2):
        pack_x(0, half)
    start(first_xy, (0, 1))

    loads[2].wait()
    loads[3].wait()
    rates = jnp.concatenate([rate_ref[...], rate_ref[...]], axis=1)
    counts = jnp.concatenate([steps_ref[...], steps_ref[...]], axis=1)
    tap = (lax.broadcasted_iota(jnp.int32, (32, 128), 0) == 0).astype(F32)
    fallen = jnp.zeros((32, 128), F32)
    for s in range(SUBS):
        rate = jnp.where(s < counts, rates, 0.0)
        fallen = fallen + rate * tap
        tap = tap + rate * (pltpu.roll(tap, 1, 0) - tap)
    taps[...] = tap
    rain_taps[...] = fallen

    column = jnp.where(low, 0, 64)

    def spread(v, index):
        return jnp.take_along_axis(v, index, axis=1)

    def speeds_x():
        right = 0.5 * (winds[pl.ds(8, 8), :] + winds[pl.ds(9, 8), :])
        left = jnp.broadcast_to(0.5 * (winds[pl.ds(7, 1), :] + winds[pl.ds(8, 1), :]), (8, 128))

        def body(z, carry):
            for yi in range(4):
                index = column + (16 * yi + z)
                row = z * 4 + yi
                speed_x[pl.ds(64 + row, 8, stride=64), :] = spread(right, index)
                speed_x[pl.ds(row, 1), :] = spread(left, index)[0:1, :]
            return carry

        lax.fori_loop(0, 16, body, 0, unroll=2)

    def speeds_y():
        own, before, after = (winds[pl.ds(24 + k, 8), :] for k in (8, 0, 16))
        following = jnp.where(lane < 112, pltpu.roll(own, 112, 1), pltpu.roll(after, 112, 1))
        right = 0.5 * (own + following)
        left = 0.5 * (own + pltpu.roll(before, 16, 1))

        def body(z, carry):
            first_face = jnp.where(
                low,
                spread(left, jnp.zeros_like(lane) + z),
                spread(right, jnp.zeros_like(lane) + (48 + z)),
            )
            speed_y[pl.ds(pl.multiple_of(z * 40, 8), 8), :] = first_face
            for k in range(1, 5):
                speed_y[pl.ds(pl.multiple_of(z * 40 + k * 8, 8), 8), :] = spread(
                    right, column + (16 * (k - 1) + z)
                )
            return carry

        lax.fori_loop(0, 16, body, 0, unroll=2)

    def speeds_z():
        own = winds[pl.ds(56, 8), :]
        right = 0.5 * (own + pltpu.roll(own, 127, 1))

        def body(z, carry):
            for yi in range(4):
                speed_z[pl.ds(pl.multiple_of(32 + z * 32 + yi * 8, 8), 8), :] = spread(
                    right, column + (16 * yi + z)
                )
            return carry

        lax.fori_loop(0, 15, body, 0, unroll=3)

    def speeds_bottom():
        left = 0.5 * (winds[pl.ds(56, 8), :] + pltpu.roll(winds[pl.ds(48, 8), :], 113, 1))
        for yi in range(4):
            speed_z[pl.ds(yi * 8, 8), :] = spread(left, column + 16 * yi)

    def speeds_top():
        right = 0.5 * (winds[pl.ds(56, 8), :] + pltpu.roll(winds[pl.ds(64, 8), :], 15, 1))
        for yi in range(4):
            speed_z[pl.ds(512 + yi * 8, 8), :] = spread(right, column + (16 * yi + 15))

    speeds_z()
    finish_recv(wind_copies, (0, 1))
    speeds_x()
    finish_recv(wind_copies, (2, 3))
    speeds_y()
    finish_recv(first_xy, (0, 1))
    for half in range(2):
        pass_x(0, half)
    finish_recv(first_xy, (2, 3))
    for half in range(2):
        unpack_y(0, half)
        pass_y(0, half)
    recv_near(wind_copies)
    when(even, speeds_top)
    when(odd, speeds_bottom)
    recv_near(first_z)
    pass_z(0, 3 * near_half, 13)

    second_z = halos_z(1)
    second_near = halos_xy(1, 1, near_half, 1)
    second_far = halos_xy(1, 2, far_half, 1)
    start_near(second_z)
    pack_y(1, near_half)
    start(second_near, (2, 3))
    pack_x(1, near_half)
    start(second_near, (0, 1))

    recv_far(wind_copies)
    when(even, speeds_bottom)
    when(odd, speeds_top)
    recv_far(first_z)
    pass_z(0, 13 * far_half, 3)
    start_far(second_z)
    pack_y(1, far_half)
    start(second_far, (2, 3))
    pack_x(1, far_half)
    start(second_far, (0, 1))

    def sed_copy(kind, yi):
        source, target = ((0, 16), (8, 24), (16, 32))[kind]
        return copy_of(
            levels.at[pl.ds(yi * COLUMN + source * 8, 64)],
            levels.at[pl.ds(yi * COLUMN + target * 8, 64)],
            sed_send.at[yi, kind], sed_recv.at[yi, kind], sides[4][1],
        )

    above = gz < nz - 1
    above_two = gz < nz - 2
    below = gz > 0
    hands_on = jnp.logical_and(below, above)

    def sed_start(kind):
        for yi in range(4):
            when(below, sed_copy(kind, yi).start)

    finish_recv(second_near, (0, 1))
    pass_x(1, near_half)
    finish_recv(second_near, (2, 3))
    unpack_y(1, near_half)
    pass_y(1, near_half)
    recv_near(second_z)
    pass_z(1, 8 * near_half, 8)
    when(even, lambda: sed_start(1))
    when(odd, lambda: sed_start(0))

    finish_recv(second_far, (0, 1))
    pass_x(1, far_half)
    finish_recv(second_far, (2, 3))
    unpack_y(1, far_half)
    pass_y(1, far_half)
    recv_far(second_z)
    pass_z(1, 8 * far_half, 8)
    when(even, lambda: sed_start(0))
    when(odd, lambda: sed_start(1))

    for yi in range(4):
        when(above, sed_copy(0, yi).wait_recv)
        when(hands_on, sed_copy(2, yi).start)

    def rain_copy(step):
        return copy_of(
            rain, rain, rain_send.at[step - 1], rain_recv.at[step - 1],
            {"gz": lax.rem(gz + step, nz)},
        )

    lowest = gz == 0
    sends_far = jnp.logical_and(even, above_two)
    follows = jnp.logical_and(even, gz > 0)

    def rain_make():
        def body(yi, carry):
            total = jnp.zeros((8, 128), F32)
            for m in range(SUBS):
                at = pl.ds(pl.multiple_of(yi * COLUMN + m * 8, 8), 8)
                total = total + rain_taps[pl.ds(m, 1), :] * levels[at, :]
            rain[pl.ds(pl.multiple_of(yi * 8, 8), 8), :] = total
            return carry

        lax.fori_loop(0, 4, body, 0)

    def rain_pass():
        rain_copy(1).start()
        when(sends_far, rain_copy(2).start)

    def rain_first():
        rain_make()
        rain_pass()

    def rain_forward():
        rain_copy(2).wait_recv()
        rain_pass()

    when(lowest, rain_first)

    loads[4].wait()
    loads[5].wait()

    def settle(u, group):
        def body(k2, carry):
            base = pl.multiple_of((2 * u + k2) * COLUMN + group * 64, 64)
            sums = [None] * 8
            for j in range(8 + SUBS):
                v = levels[pl.ds(base + j * 8, 8), :]
                for k in range(8):
                    if 0 <= j - k <= SUBS:
                        term = taps[pl.ds(j - k, 1), :] * v
                        sums[k] = term if sums[k] is None else sums[k] + term
            for k in range(8):
                stage[pl.ds(pl.multiple_of(k2 * 64 + k * 8, 8), 8), :] = sums[k]
            return carry

        lax.fori_loop(0, 2, body, 0)

    def breakup(u, group):
        block = jnp.concatenate(
            [stage[pl.ds(k2 * 64 + x, 8, stride=8), :] for k2 in range(2) for x in range(8)], axis=0
        ).T
        for h in range(2):
            cells[:, 128 * h : 128 * h + 128] = block[64 * h : 64 * h + 64]
        small = cells[...].astype(BF16)
        rounded[...] = small.astype(F32)

        def body(i, total):
            wide = rounded[...]
            terms = [rounded[pl.ds(i * 4 + k, 1), :] * wide for k in range(4)]
            block = jnp.concatenate(terms, axis=0).astype(BF16)
            part = gains[:, pl.ds(pl.multiple_of(i * 256, 256), 256)]
            return total + jnp.dot(part, block, preferred_element_type=F32)

        loss = lax.dot_general(
            collide_ref[...], small, (((0,), (0,)), ((), ())), preferred_element_type=F32
        )
        gained = lax.fori_loop(0, 16, body, jnp.zeros((64, 256), F32), unroll=4)
        settled = cells[...]
        result = settled + gained - settled * loss
        for h in range(2):
            back = result[:, 128 * h : 128 * h + 128].T
            for k2 in range(2):
                out_ref[:, 4 * h + 2 * u + k2, 8 * group : 8 * group + 8, :] = back[
                    64 * k2 : 64 * k2 + 64
                ].reshape(8, 8, 64)

    for u in range(2):
        for yi in (2 * u, 2 * u + 1):
            when(above, sed_copy(1, yi).wait_recv)
        settle(u, 0)
        breakup(u, 0)
    when(follows, rain_forward)
    for u in range(2):
        for yi in (2 * u, 2 * u + 1):
            when(above_two, sed_copy(2, yi).wait_recv)
        settle(u, 1)
        breakup(u, 1)

    when(odd, rain_copy(1).wait_recv)
    mine = rain[pl.ds(pl.multiple_of(lax.rem(gz, 4) * 8, 8), 8), :]
    upper = (jnp.zeros((8, 128), jnp.int32) + gz) >= 4
    rain_ref[:, 0, :] = jnp.where(upper, turn(mine), mine)[:, :64]

    when(even, rain_copy(1).wait_send)
    when(sends_far, rain_copy(2).wait_send)
    for yi in range(4):
        when(below, sed_copy(0, yi).wait_send)
        when(below, sed_copy(1, yi).wait_send)
        when(hands_on, sed_copy(2, yi).wait_send)
    finish_send(wind_copies)
    for copies in (first_z, first_xy, second_z, second_near, second_far):
        finish_send(copies)


def per_device(sizes, bin_mass, courant, sub_courant, fall_steps, frag_gain, collide):
    vmem, dma = pltpu.VMEM, pltpu.SemaphoreType.DMA
    out, rain = pl.pallas_call(
        functools.partial(kernel, *sizes),
        out_shape=(
            jax.ShapeDtypeStruct((8, 8, 16, 64), F32),
            jax.ShapeDtypeStruct((8, 1, 64), F32),
        ),
        in_specs=[pl.BlockSpec(memory_space=pl.ANY)] * 6,
        out_specs=(pl.BlockSpec(memory_space=vmem), pl.BlockSpec(memory_space=vmem)),
        scratch_shapes=[
            vmem((1024, 64), F32),
            vmem((3, 8, 8, 16), F32),
            vmem((1, 64), F32),
            vmem((1, 64), jnp.int32),
            vmem((64, 4096), BF16),
            vmem((64, 64), BF16),
            vmem((2 * FIELD, 128), F32),
            vmem((512, 128), F32),
            vmem((384, 128), F32),
            vmem((256, 128), F32),
            vmem((640, 128), F32),
            vmem((384, 128), F32),
            vmem((256, 128), F32),
            vmem((640, 128), F32),
            vmem((640, 128), F32),
            vmem((72, 128), F32),
            vmem((9 * 64, 128), F32),
            vmem((16 * 40, 128), F32),
            vmem((17 * 32, 128), F32),
            vmem((32, 128), F32),
            vmem((32, 128), F32),
            vmem((4 * COLUMN, 128), F32),
            vmem((128, 128), F32),
            vmem((64, 256), F32),
            vmem((64, 256), F32),
            vmem((32, 128), F32),
            dma((6,)),
            dma((3, 6)),
            dma((3, 6)),
            dma((6,)),
            dma((6,)),
            dma((4, 3)),
            dma((4, 3)),
            dma((2,)),
            dma((2,)),
        ],
        compiler_params=pltpu.CompilerParams(
            collective_id=0, has_side_effects=True, vmem_limit_bytes=60 << 20
        ),
    )(
        bin_mass.reshape(1024, 64),
        courant,
        sub_courant.reshape(1, 64),
        fall_steps.reshape(1, 64),
        frag_gain.T,
        collide,
    )
    return out, rain


def solution(mesh):
    in_specs = (P("gx", "gy", "gz", None), P(None, "gx", "gy", "gz"), P(), P(), P(), P())
    out_specs = (P("gx", "gy", "gz", None), P("gx", ("gy", "gz"), None))
    sizes = tuple(mesh.shape[a] for a in ("gx", "gy", "gz"))
    return jax.shard_map(
        functools.partial(per_device, sizes),
        mesh=mesh,
        in_specs=in_specs,
        out_specs=out_specs,
        check_vma=False,
    )
```

time: 59.9 us -> 50.3 us (0.84)
  the two profiles are of different devices: /device:TPU:25 before, /device:TPU:35 now
where the time goes in v2:
time: 50.3 us; the launch traced here: 50.2 us
  Pallas kernels  47 us (93%)
  local copies, waits for them, and re-layouts  2.47 us (5%)
  between operations  0.65 us (1%)
    pallas_call x1, Pallas kernels, per_device(): pl.pallas_call(functools.partial(kernel, *sizes), out_shape=(jax.ShapeDty...  47 us
    unnamed x4, local copies, waits for them, and re-layouts  2.47 us

profile of v2, /device:TPU:35, one launch (start us, length us, event | category | flops | bytes accessed | tf_op | source)
XLA Modules:
  0.0 50.2 jit_solution(8799276216407390022)
XLA Ops:
  0.6 47.0 %shard_map.77 = (f32[8,8,16,64]{3,2,1,0:T(8,128)}, f32[8,1,64]{2,1,0:T(1,128)}) custom-call(f32[1024,64]{1,0:T(8,128)} %bitcast.4, f32[3,8,8,16]{3,2,1,0:T(8,128)} %courant_hbm.1, f32[1,64]{1,0:T(1,128)} %bitcast.6, s32[1,64]{1,0:T(1,128)} %bitcast.7, bf16[64,4096]{1,0:T(8,128)(2,1)} %bitcast.5, bf16[64,64]{1,0:T(8,128)(2,1)} %collide_hbm.1), custom_call_target="tpu_custom_call" | custom-call | tf_op jit(solution)/shard_map/pallas_call | solution.py:661
  47.7 0.0 copy-start
  47.7 1.9 %copy.10 = f32[8,8,16,64]{3,2,1,0:T(8,128)} copy(f32[8,8,16,64]{3,2,1,0:T(8,128)} %get-tuple-element.4) | data formatting | bytes 524288
  49.6 0.0 copy-done
  49.6 0.6 %copy.11 = f32[8,1,64]{2,1,0:T(1,128)} copy(f32[8,1,64]{2,1,0:T(1,128)S(1)} %copy-done) | data formatting | bytes 4096
Async XLA Ops:
  47.7 1.9 %copy-start = (f32[8,1,64]{2,1,0:T(1,128)S(1)}, f32[8,1,64]{2,1,0:T(1,128)}, u32[]{:S(2)}) copy-start(f32[8,1,64]{2,1,0:T(1,128)} %get-tuple-element.5) | copy-start | bytes 6148

commit v3 on v2

--- a/solution.py
+++ b/solution.py
@@ -70,8 +70,9 @@
     mass_hbm, courant_hbm, rate_hbm, steps_hbm, gain_hbm, collide_hbm,
     out_ref, rain_ref,
     raw, courant_ref, rate_ref, steps_ref, gains, collide_ref, field, tend, x_low, x_high, x_out, y_low, y_high, y_out, y_in, winds,
-    speed_x, speed_y, speed_z, taps, rain_taps, levels, stage, cells, rounded, rain,
+    speed_x, speed_y, speed_z, taps, rain_taps, levels, stage, cells, rounded, rain, done, rain_done,
     load_sem, halo_send, halo_recv, wind_send, wind_recv, sed_send, sed_recv, rain_send, rain_recv,
+    store_sem,
 ):
     gx, gy, gz = lax.axis_index("gx"), lax.axis_index("gy"), lax.axis_index("gz")
     parity = lax.rem(gz, 2)
@@ -302,7 +303,7 @@
                 y_high[pl.ds(pl.multiple_of(at, 8), 8), :] = jnp.where(low, own_a, turn(got))
                 y_high[pl.ds(pl.multiple_of(at + 64, 8), 8), :] = jnp.where(low, own_b, got)
 
-    def pass_x(s, half):
+    def pass_x(s, half, fresh):
         base = s * FIELD + OWN
 
         def body(q, carry):
@@ -321,18 +322,19 @@
                 return speed_x[pl.ds(pl.multiple_of(k * 64 + at, 8), 16), :]
 
             def emit(i, change):
-                tend[pl.ds(at * 8 + i, 16, stride=8), :] = -change
+                to = pl.ds(at * 8 + i, 16, stride=8)
+                tend[to, :] = -change if fresh else tend[to, :] - change
 
             weno_line(8, value, speed, emit)
             return carry
 
         lax.fori_loop(0, 2, body, 0)
 
-    def pass_y(s, half):
+    def pass_y(s, first_level, count, last):
         base = s * FIELD + OWN
 
-        def body(zi, carry):
-            z = half * 8 + zi
+        def body(k, carry):
+            z = first_level + k
 
             def value(i):
                 if i < 0:
@@ -345,15 +347,27 @@
                 return speed_y[pl.ds(pl.multiple_of((z * 5 + k) * 8, 8), 8), :]
 
             def emit(i, change):
-                at = pl.ds(pl.multiple_of(z * 32 + i * 8, 8), 8)
-                tend[at, :] = tend[at, :] - change
+                row = z * 32 + i * 8
+                at = pl.ds(pl.multiple_of(row, 8), 8)
+                total = tend[at, :] - change
+                if not last:
+                    tend[at, :] = total
+                    return
+                stepped = value(i) + total
+                if s == 0:
+                    field[pl.ds(pl.multiple_of(FIELD + OWN + row, 8), 8), :] = stepped
+                else:
+                    before = field[pl.ds(pl.multiple_of(OWN + row, 8), 8), :]
+                    to = pl.ds(pl.multiple_of(i * COLUMN + z * 8, 8), 8)
+                    levels[to, :] = 0.5 * before + 0.5 * stepped
 
             weno_line(4, value, speed, emit)
             return carry
 
-        lax.fori_loop(0, 8, body, 0, unroll=2)
-
-    def pass_z(s, first_level, count):
+        unroll = 2 if count % 2 == 0 else 1
+        lax.fori_loop(0, count, body, 0, unroll=unroll)
+
+    def pass_z(s, first_level, count, last):
         for p in range(2):
             at = first_level * 32 + p * 16
 
@@ -365,6 +379,9 @@
 
             def emit(i, change):
                 row = i * 32 + at
+                if not last:
+                    tend[pl.ds(pl.multiple_of(row, 8), 16), :] = -change
+                    return
                 stepped = value(i) + (tend[pl.ds(pl.multiple_of(row, 8), 16), :] - change)
                 if s == 0:
                     field[pl.ds(pl.multiple_of(FIELD + OWN + row, 8), 16), :] = stepped
@@ -471,18 +488,18 @@
     speeds_x()
     finish_recv(wind_copies, (2, 3))
     speeds_y()
+    recv_near(wind_copies)
+    when(even, speeds_top)
+    when(odd, speeds_bottom)
     finish_recv(first_xy, (0, 1))
     for half in range(2):
-        pass_x(0, half)
+        pass_x(0, half, True)
     finish_recv(first_xy, (2, 3))
     for half in range(2):
         unpack_y(0, half)
-        pass_y(0, half)
-    recv_near(wind_copies)
-    when(even, speeds_top)
-    when(odd, speeds_bottom)
+    pass_y(0, 0, 16, False)
     recv_near(first_z)
-    pass_z(0, 3 * near_half, 13)
+    pass_z(0, 3 * near_half, 13, True)
 
     second_z = halos_z(1)
     second_near = halos_xy(1, 1, near_half, 1)
@@ -497,7 +514,7 @@
     when(even, speeds_bottom)
     when(odd, speeds_top)
     recv_far(first_z)
-    pass_z(0, 13 * far_half, 3)
+    pass_z(0, 13 * far_half, 3, True)
     start_far(second_z)
     pack_y(1, far_half)
     start(second_far, (2, 3))
@@ -507,8 +524,8 @@
     def sed_copy(kind, yi):
         source, target = ((0, 16), (8, 24), (16, 32))[kind]
         return copy_of(
-            levels.at[pl.ds(yi * COLUMN + source * 8, 64)],
-            levels.at[pl.ds(yi * COLUMN + target * 8, 64)],
+            levels.at[pl.ds(pl.multiple_of(yi * COLUMN + source * 8, 64), 64)],
+            levels.at[pl.ds(pl.multiple_of(yi * COLUMN + target * 8, 64), 64)],
             sed_send.at[yi, kind], sed_recv.at[yi, kind], sides[4][1],
         )
 
@@ -522,28 +539,36 @@
             when(below, sed_copy(kind, yi).start)
 
     finish_recv(second_near, (0, 1))
-    pass_x(1, near_half)
+    pass_x(1, near_half, True)
     finish_recv(second_near, (2, 3))
     unpack_y(1, near_half)
-    pass_y(1, near_half)
+    pass_y(1, 8 * near_half, 8, False)
     recv_near(second_z)
-    pass_z(1, 8 * near_half, 8)
+    pass_z(1, 8 * near_half, 8, True)
     when(even, lambda: sed_start(1))
     when(odd, lambda: sed_start(0))
 
     finish_recv(second_far, (0, 1))
-    pass_x(1, far_half)
+    pass_x(1, far_half, True)
     finish_recv(second_far, (2, 3))
     unpack_y(1, far_half)
-    pass_y(1, far_half)
+    pass_y(1, 8 * far_half, 8, False)
     recv_far(second_z)
-    pass_z(1, 8 * far_half, 8)
-    when(even, lambda: sed_start(0))
+    pass_z(1, 8 * far_half, 8, True)
+
+    def hand_on(u):
+        for k in range(2):
+            when(above, sed_copy(0, 2 * u + k).wait_recv)
+            when(hands_on, sed_copy(2, 2 * u + k).start)
+
+    def far_even():
+        for yi in range(4):
+            when(below, sed_copy(0, yi).start)
+        for u in range(2):
+            hand_on(u)
+
+    when(even, far_even)
     when(odd, lambda: sed_start(1))
-
-    for yi in range(4):
-        when(above, sed_copy(0, yi).wait_recv)
-        when(hands_on, sed_copy(2, yi).start)
 
     def rain_copy(step):
         return copy_of(
@@ -624,26 +649,48 @@
         for h in range(2):
             back = result[:, 128 * h : 128 * h + 128].T
             for k2 in range(2):
-                out_ref[:, 4 * h + 2 * u + k2, 8 * group : 8 * group + 8, :] = back[
-                    64 * k2 : 64 * k2 + 64
-                ].reshape(8, 8, 64)
-
-    for u in range(2):
-        for yi in (2 * u, 2 * u + 1):
-            when(above, sed_copy(1, yi).wait_recv)
-        settle(u, 0)
-        breakup(u, 0)
-    when(follows, rain_forward)
-    for u in range(2):
-        for yi in (2 * u, 2 * u + 1):
-            when(above_two, sed_copy(2, yi).wait_recv)
-        settle(u, 1)
-        breakup(u, 1)
+                done[
+                    :, pl.ds(4 * h + 2 * u + k2, 1), pl.ds(pl.multiple_of(8 * group, 8), 8), :
+                ] = back[64 * k2 : 64 * k2 + 64].reshape(8, 1, 8, 64)
+
+    def unit_of(t):
+        outer, inner = t // 2, t % 2
+        return parity * outer + (1 - parity) * inner, parity * inner + (1 - parity) * outer
+
+    def store(t, h):
+        u, group = unit_of(t)
+        where = (
+            slice(None),
+            pl.ds(4 * h + 2 * u, 2),
+            pl.ds(pl.multiple_of(8 * group, 8), 8),
+            slice(None),
+        )
+        return pltpu.make_async_copy(done.at[where], out_ref.at[where], store_sem.at[t, h])
+
+    def both(a, b):
+        return jnp.logical_and(a, b)
+
+    for t in range(4):
+        u, group = unit_of(t)
+        if t % 2 == 0:
+            when(odd, lambda u=u: hand_on(u))
+        for k in range(2):
+            when(both(group == 0, above), sed_copy(1, 2 * u + k).wait_recv)
+        if t == 2:
+            when(follows, rain_forward)
+        for k in range(2):
+            when(both(group == 1, above_two), sed_copy(2, 2 * u + k).wait_recv)
+        settle(u, group)
+        breakup(u, group)
+        for h in range(2):
+            store(t, h).start()
 
     when(odd, rain_copy(1).wait_recv)
     mine = rain[pl.ds(pl.multiple_of(lax.rem(gz, 4) * 8, 8), 8), :]
     upper = (jnp.zeros((8, 128), jnp.int32) + gz) >= 4
-    rain_ref[:, 0, :] = jnp.where(upper, turn(mine), mine)[:, :64]
+    rain_done[:, 0, :] = jnp.where(upper, turn(mine), mine)[:, :64]
+    rain_store = pltpu.make_async_copy(rain_done, rain_ref, load_sem.at[0])
+    rain_store.start()
 
     when(even, rain_copy(1).wait_send)
     when(sends_far, rain_copy(2).wait_send)
@@ -652,8 +699,27 @@
         when(below, sed_copy(1, yi).wait_send)
         when(hands_on, sed_copy(2, yi).wait_send)
     finish_send(wind_copies)
+    for t in range(4):
+        for h in range(2):
+            store(t, h).wait()
+    rain_store.wait()
     for copies in (first_z, first_xy, second_z, second_near, second_far):
         finish_send(copies)
+
+
+def hand_over(mass_ref, fall_ref, out_ref, rain_ref, mass, fall, sem):
+    reads = [pltpu.make_async_copy(fall_ref, fall, sem.at[0, 8])]
+    writes = [pltpu.make_async_copy(fall, rain_ref, sem.at[1, 8])]
+    for k in range(8):
+        reads.append(pltpu.make_async_copy(mass_ref.at[k], mass.at[k], sem.at[0, k]))
+        writes.append(pltpu.make_async_copy(mass.at[k], out_ref.at[k], sem.at[1, k]))
+    for copy in reads:
+        copy.start()
+    for read, write in zip(reads, writes):
+        read.wait()
+        write.start()
+    for copy in writes:
+        copy.wait()
 
 
 def per_device(sizes, bin_mass, courant, sub_courant, fall_steps, frag_gain, collide):
@@ -665,7 +731,7 @@
             jax.ShapeDtypeStruct((8, 1, 64), F32),
         ),
         in_specs=[pl.BlockSpec(memory_space=pl.ANY)] * 6,
-        out_specs=(pl.BlockSpec(memory_space=vmem), pl.BlockSpec(memory_space=vmem)),
+        out_specs=(pl.BlockSpec(memory_space=pl.ANY), pl.BlockSpec(memory_space=pl.ANY)),
         scratch_shapes=[
             vmem((1024, 64), F32),
             vmem((3, 8, 8, 16), F32),
@@ -693,6 +759,8 @@
             vmem((64, 256), F32),
             vmem((64, 256), F32),
             vmem((32, 128), F32),
+            vmem((8, 8, 16, 64), F32),
+            vmem((8, 1, 64), F32),
             dma((6,)),
             dma((3, 6)),
             dma((3, 6)),
@@ -702,6 +770,7 @@
             dma((4, 3)),
             dma((2,)),
             dma((2,)),
+            dma((4, 2)),
         ],
         compiler_params=pltpu.CompilerParams(
             collective_id=0, has_side_effects=True, vmem_limit_bytes=60 << 20
@@ -714,7 +783,17 @@
         frag_gain.T,
         collide,
     )
-    return out, rain
+    return pl.pallas_call(
+        hand_over,
+        out_shape=(
+            jax.ShapeDtypeStruct((8, 8, 16, 64), F32),
+            jax.ShapeDtypeStruct((8, 1, 64), F32),
+        ),
+        in_specs=[pl.BlockSpec(memory_space=pl.ANY)] * 2,
+        out_specs=(pl.BlockSpec(memory_space=pl.ANY), pl.BlockSpec(memory_space=pl.ANY)),
+        scratch_shapes=[vmem((8, 8, 16, 64), F32), vmem((8, 1, 64), F32), dma((2, 9))],
+        compiler_params=pltpu.CompilerParams(vmem_limit_bytes=60 << 20),
+    )(out, rain)
 
 
 def solution(mesh):

time: 50.3 us -> 49 us (0.974)
  local copies, waits for them, and re-layouts: 2.47 us -> 0 us
  Pallas kernels: 47 us -> 48.1 us
    unnamed x4 -> x0, local copies, waits for them, and re-layouts: 2.47 us -> none
    pallas_call x0 -> x1, Pallas kernels: none -> 1.85 us  [per_device(): pl.pallas_call(hand_over, out_shape=(jax.ShapeDtypeStruct((8, 8, 16, 64),...]
    pallas_call x1, Pallas kernels: 47 us -> 46.3 us  [per_device(): pl.pallas_call(functools.partial(kernel, *sizes), out_shape=(jax.ShapeDty...]
where the time goes in v3:
time: 49 us; the launch traced here: 48.8 us
  Pallas kernels  48.1 us (98%)
  between operations  0.64 us (1%)
    pallas_call x1, Pallas kernels, per_device(): pl.pallas_call(functools.partial(kernel, *sizes), out_shape=(jax.ShapeDty...  46.3 us
    pallas_call x1, Pallas kernels, per_device(): pl.pallas_call(hand_over, out_shape=(jax.ShapeDtypeStruct((8, 8, 16, 64),...  1.85 us

profile of v3, /device:TPU:35, one launch (start us, length us, event | category | flops | bytes accessed | tf_op | source)
XLA Modules:
  0.0 48.8 jit_solution(6641033202232590092)
XLA Ops:
  0.6 46.3 %shard_map.77 = (f32[8,8,16,64]{3,2,1,0:T(8,128)}, f32[8,1,64]{2,1,0:T(1,128)}) custom-call(f32[1024,64]{1,0:T(8,128)} %bitcast.4, f32[3,8,8,16]{3,2,1,0:T(8,128)} %courant_hbm.1, f32[1,64]{1,0:T(1,128)} %bitcast.6, s32[1,64]{1,0:T(1,128)} %bitcast.7, bf16[64,4096]{1,0:T(8,128)(2,1)} %bitcast.5, bf16[64,64]{1,0:T(8,128)(2,1)} %collide_hbm.1), custom_call_target="tpu_custom_call" | custom-call | tf_op jit(solution)/shard_map/pallas_call | solution.py:727
  46.9 1.9 %shard_map.78 = (f32[8,8,16,64]{3,2,1,0:T(8,128)}, f32[8,1,64]{2,1,0:T(1,128)}) custom-call(f32[8,8,16,64]{3,2,1,0:T(8,128)} %get-tuple-element.4.mass_ref, f32[8,1,64]{2,1,0:T(1,128)} %get-tuple-element.5.fall_ref), custom_call_target="tpu_custom_call" | custom-call | tf_op jit(solution)/shard_map/pallas_call | solution.py:786

commit v4 on v3

--- a/solution.py
+++ b/solution.py
@@ -174,7 +174,7 @@
             )
         return carry
 
-    lax.fori_loop(0, 16, pack, 0, unroll=2)
+    lax.fori_loop(0, 16, pack, 0, unroll=8)
 
     loads[1].wait()
     for d in range(3):
@@ -328,7 +328,7 @@
             weno_line(8, value, speed, emit)
             return carry
 
-        lax.fori_loop(0, 2, body, 0)
+        lax.fori_loop(0, 2, body, 0, unroll=2)
 
     def pass_y(s, first_level, count, last):
         base = s * FIELD + OWN
@@ -407,19 +407,6 @@
         pack_x(0, half)
     start(first_xy, (0, 1))
 
-    loads[2].wait()
-    loads[3].wait()
-    rates = jnp.concatenate([rate_ref[...], rate_ref[...]], axis=1)
-    counts = jnp.concatenate([steps_ref[...], steps_ref[...]], axis=1)
-    tap = (lax.broadcasted_iota(jnp.int32, (32, 128), 0) == 0).astype(F32)
-    fallen = jnp.zeros((32, 128), F32)
-    for s in range(SUBS):
-        rate = jnp.where(s < counts, rates, 0.0)
-        fallen = fallen + rate * tap
-        tap = tap + rate * (pltpu.roll(tap, 1, 0) - tap)
-    taps[...] = tap
-    rain_taps[...] = fallen
-
     column = jnp.where(low, 0, 64)
 
     def spread(v, index):
@@ -437,7 +424,7 @@
                 speed_x[pl.ds(row, 1), :] = spread(left, index)[0:1, :]
             return carry
 
-        lax.fori_loop(0, 16, body, 0, unroll=2)
+        lax.fori_loop(0, 16, body, 0, unroll=8)
 
     def speeds_y():
         own, before, after = (winds[pl.ds(24 + k, 8), :] for k in (8, 0, 16))
@@ -458,7 +445,7 @@
                 )
             return carry
 
-        lax.fori_loop(0, 16, body, 0, unroll=2)
+        lax.fori_loop(0, 16, body, 0, unroll=8)
 
     def speeds_z():
         own = winds[pl.ds(56, 8), :]
@@ -471,7 +458,7 @@
                 )
             return carry
 
-        lax.fori_loop(0, 15, body, 0, unroll=3)
+        lax.fori_loop(0, 15, body, 0, unroll=5)
 
     def speeds_bottom():
         left = 0.5 * (winds[pl.ds(56, 8), :] + pltpu.roll(winds[pl.ds(48, 8), :], 113, 1))
@@ -538,6 +525,19 @@
         for yi in range(4):
             when(below, sed_copy(kind, yi).start)
 
+    loads[2].wait()
+    loads[3].wait()
+    rates = jnp.concatenate([rate_ref[...], rate_ref[...]], axis=1)
+    counts = jnp.concatenate([steps_ref[...], steps_ref[...]], axis=1)
+    tap = (lax.broadcasted_iota(jnp.int32, (32, 128), 0) == 0).astype(F32)
+    fallen = jnp.zeros((32, 128), F32)
+    for s in range(SUBS):
+        rate = jnp.where(s < counts, rates, 0.0)
+        fallen = fallen + rate * tap
+        tap = tap + rate * (pltpu.roll(tap, 1, 0) - tap)
+    taps[...] = tap
+    rain_taps[...] = fallen
+
     finish_recv(second_near, (0, 1))
     pass_x(1, near_half, True)
     finish_recv(second_near, (2, 3))
@@ -622,7 +622,7 @@
                 stage[pl.ds(pl.multiple_of(k2 * 64 + k * 8, 8), 8), :] = sums[k]
             return carry
 
-        lax.fori_loop(0, 2, body, 0)
+        lax.fori_loop(0, 2, body, 0, unroll=2)
 
     def breakup(u, group):
         block = jnp.concatenate(
@@ -643,7 +643,7 @@
         loss = lax.dot_general(
             collide_ref[...], small, (((0,), (0,)), ((), ())), preferred_element_type=F32
         )
-        gained = lax.fori_loop(0, 16, body, jnp.zeros((64, 256), F32), unroll=4)
+        gained = lax.fori_loop(0, 16, body, jnp.zeros((64, 256), F32), unroll=16)
         settled = cells[...]
         result = settled + gained - settled * loss
         for h in range(2):

time: 49 us -> 48.1 us (0.982)
  Pallas kernels: 48.1 us -> 47.2 us
    pallas_call x1, Pallas kernels: 46.3 us -> 45.4 us  [per_device(): pl.pallas_call(functools.partial(kernel, *sizes), out_shape=(jax.ShapeDty...]
where the time goes in v4:
time: 48.1 us; the launch traced here: 47.9 us
  Pallas kernels  47.2 us (98%)
  between operations  0.64 us (1%)
    pallas_call x1, Pallas kernels, per_device(): pl.pallas_call(functools.partial(kernel, *sizes), out_shape=(jax.ShapeDty...  45.4 us
    pallas_call x1, Pallas kernels, per_device(): pl.pallas_call(hand_over, out_shape=(jax.ShapeDtypeStruct((8, 8, 16, 64),...  1.85 us

profile of v4, /device:TPU:35, one launch (start us, length us, event | category | flops | bytes accessed | tf_op | source)
XLA Modules:
  0.0 47.9 jit_solution(1878370446033496093)
XLA Ops:
  0.6 45.4 %shard_map.77 = (f32[8,8,16,64]{3,2,1,0:T(8,128)}, f32[8,1,64]{2,1,0:T(1,128)}) custom-call(f32[1024,64]{1,0:T(8,128)} %bitcast.4, f32[3,8,8,16]{3,2,1,0:T(8,128)} %courant_hbm.1, f32[1,64]{1,0:T(1,128)} %bitcast.6, s32[1,64]{1,0:T(1,128)} %bitcast.7, bf16[64,4096]{1,0:T(8,128)(2,1)} %bitcast.5, bf16[64,64]{1,0:T(8,128)(2,1)} %collide_hbm.1), custom_call_target="tpu_custom_call" | custom-call | tf_op jit(solution)/shard_map/pallas_call | solution.py:727
  46.0 1.9 %shard_map.78 = (f32[8,8,16,64]{3,2,1,0:T(8,128)}, f32[8,1,64]{2,1,0:T(1,128)}) custom-call(f32[8,8,16,64]{3,2,1,0:T(8,128)} %get-tuple-element.4.mass_ref, f32[8,1,64]{2,1,0:T(1,128)} %get-tuple-element.5.fall_ref), custom_call_target="tpu_custom_call" | custom-call | tf_op jit(solution)/shard_map/pallas_call | solution.py:786
